TPU v7x, 32 devices: a whole 2x2x4 slice. The times are simulated.
32 devices in a mesh: dp: 4 (over y, x), mp: 8 (over z, core).
Axes of the slice: x: 2, y: 2, z: 4, core: 2. Of those that a mesh axis runs over, the one named last changes fastest.
Arguments:
- queries: bfloat16 [3, 2048, 4096], P(None, 'dp', 'mp'), may hold values from -15 to 15
- memory: bfloat16 [128, 4096], P('mp'), may hold values from -6 to 6
- w_key: bfloat16 [3, 4096, 4096], P(None, 'mp'), may hold values from -0.09375 to 0.09375
- w_value: bfloat16 [3, 4096, 4096], P(None, 'mp'), may hold values from -0.09375 to 0.09375
- grad_out: bfloat16 [3, 2048, 4096], P(None, 'dp', 'mp'), may hold values from -6 to 6
Outputs:
- attended: bfloat16 [3, 2048, 4096], P(None, 'dp', 'mp')
- grad_queries: bfloat16 [3, 2048, 4096], P(None, 'dp', 'mp')
- grad_memory: float32 [128, 4096], P('mp')
- grad_w_key: float32 [3, 4096, 4096], P(None, 'mp')
- grad_w_value: float32 [3, 4096, 4096], P(None, 'mp')
All inputs are finite; a program needn't handle non-finite values.
Results may differ from a plain program's by a relative error of at most 0.025.
Values may be sent and summed in bfloat16 or wider, within the bound.
A program may use at most 128 MiB of HBM per device.

v0:
```python
import jax
import jax.numpy as jnp
from jax import lax
from jax.sharding import PartitionSpec as P

HEAD_WIDTH = 64


def shards(queries, memory, w_key, w_value, grad_out):
    layers, rows, width = queries.shape
    heads_dev = width // HEAD_WIDTH
    mem_all = lax.all_gather(memory, "mp", axis=0, tiled=True)
    mem_total = mem_all.shape[0]
    keys = jnp.einsum("md,lcd->lmc", mem_all, w_key, preferred_element_type=jnp.float32).astype(
        jnp.bfloat16
    )
    values = jnp.einsum("md,lcd->lmc", mem_all, w_value, preferred_element_type=jnp.float32).astype(
        jnp.bfloat16
    )
    per_head_queries = queries.reshape(layers, rows, heads_dev, HEAD_WIDTH)
    per_head_keys = keys.reshape(layers, mem_total, heads_dev, HEAD_WIDTH)
    per_head_values = values.reshape(layers, mem_total, heads_dev, HEAD_WIDTH)
    head_output_gradient = grad_out.reshape(layers, rows, heads_dev, HEAD_WIDTH)
    attention_logits = jnp.einsum(
        "lrhd,lmhd->lhrm", per_head_queries, per_head_keys, preferred_element_type=jnp.float32
    )
    row_max = jnp.max(attention_logits, axis=-1, keepdims=True)
    exp_scores = jnp.exp(attention_logits - row_max)
    attn_probs = exp_scores / jnp.sum(exp_scores, axis=-1, keepdims=True)
    batch_probabilities = attn_probs.astype(jnp.bfloat16)
    attended = (
        jnp.einsum(
            "lhrm,lmhd->lrhd",
            batch_probabilities,
            per_head_values,
            preferred_element_type=jnp.float32,
        )
        .reshape(layers, rows, width)
        .astype(jnp.bfloat16)
    )
    probability_gradient = jnp.einsum(
        "lrhd,lmhd->lhrm", head_output_gradient, per_head_values, preferred_element_type=jnp.float32
    )
    row_delta = jnp.sum(attn_probs * probability_gradient, axis=-1, keepdims=True)
    logit_gradient = (attn_probs * (probability_gradient - row_delta)).astype(jnp.bfloat16)
    grad_queries = (
        jnp.einsum(
            "lhrm,lmhd->lrhd", logit_gradient, per_head_keys, preferred_element_type=jnp.float32
        )
        .reshape(layers, rows, width)
        .astype(jnp.bfloat16)
    )
    key_part = jnp.einsum(
        "lhrm,lrhd->lmhd", logit_gradient, per_head_queries, preferred_element_type=jnp.float32
    ).reshape(layers, mem_total, width)
    value_part = jnp.einsum(
        "lhrm,lrhd->lmhd",
        batch_probabilities,
        head_output_gradient,
        preferred_element_type=jnp.float32,
    ).reshape(layers, mem_total, width)
    key_sum, value_sum = lax.psum((key_part, value_part), "dp")
    key_gradient = key_sum.astype(jnp.bfloat16)
    value_gradient = value_sum.astype(jnp.bfloat16)
    grad_w_key = jnp.einsum(
        "lmc,md->lcd", key_gradient, mem_all, preferred_element_type=jnp.float32
    )
    grad_w_value = jnp.einsum(
        "lmc,md->lcd", value_gradient, mem_all, preferred_element_type=jnp.float32
    )
    grad_memory = lax.psum_scatter(
        jnp.einsum("lmc,lcd->md", key_gradient, w_key, preferred_element_type=jnp.float32)
        + jnp.einsum("lmc,lcd->md", value_gradient, w_value, preferred_element_type=jnp.float32),
        "mp",
        scatter_dimension=0,
        tiled=True,
    )
    return (attended, grad_queries, grad_memory, grad_w_key, grad_w_value)


def solution(mesh):
    return jax.shard_map(
        shards,
        mesh=mesh,
        in_specs=(
            P(None, "dp", "mp"),
            P("mp", None),
            P(None, "mp", None),
            P(None, "mp", None),
            P(None, "dp", "mp"),
        ),
        out_specs=(
            P(None, "dp", "mp"),
            P(None, "dp", "mp"),
            P("mp", None),
            P(None, "mp", None),
            P(None, "mp", None),
        ),
        check_vma=False,
    )
```

profile of v0, /device:TPU:0, one launch (start us, length us, event | category | flops | bytes accessed | tf_op | source)
XLA Modules:
  0.0 191.2 jit_solution(15210810863167152440)
XLA Ops:
  7.2 0.0 all-gather.2.cloned.1.call-start
  7.2 0.7 all-gather.2.cloned.1.call-update
  7.9 0.0 reduce-scatter.2.cloned.1.call-start
  7.9 1.7 copy.24
  9.7 0.0 copy-start
  9.7 3.2 %copy.26 = bf16[3,512,512]{1,2,0:T(8,128)(2,1)} copy(bf16[3,512,512]{2,1,0:T(8,128)(2,1)} %param.9) | data formatting | bytes 3145728 | tf_op args[4]
  12.8 21.6 %all-gather.2.cloned.1.call-done = bf16[128,4096]{1,0:T(8,128)(2,1)} async-done(((bf16[16,4096]{1,0:T(8,128)(2,1)}), bf16[128,4096]{1,0:T(8,128)(2,1)}) %all-gather.2.cloned.1.call-update) | async-done | bytes 1048592 | tf_op jit(solution)/shard_map/all_gather | solution.py:12
  34.4 8.3 %convolution_convert_fusion.2 = bf16[3,512,128]{2,1,0:T(8,128)(2,1)S(1)} fusion(bf16[3,512,4096]{2,1,0:T(8,128)(2,1)} %param.7, bf16[128,4096]{1,0:T(8,128)(2,1)} %all-gather.2.cloned.1.call-done), kind=kOutput, calls=%fused_computation.19 | convolution fusion | flops 1610809344 | bytes 14024704 | tf_op jit(solution)/shard_map/md,lcd->lmc/dot_general | solution.py:14
  42.7 0.0 copy-start.4
  42.7 0.0 copy-done
  42.7 4.5 %fusion.24 = (f32[3,8,512]{2,1,0:T(8,128)S(1)}, f32[3,8,512,128]{2,3,1,0:T(8,128)}) fusion(bf16[3,128,8,64]{1,3,2,0:T(8,128)(2,1)S(1)} %bitcast.83, bf16[3,512,8,64]{1,3,2,0:T(8,128)(2,1)S(1)} %bitcast.79), kind=kOutput, calls=%fused_computation.32 | convolution fusion | flops 204472448 | bytes 8306688 | tf_op jit(solution)/shard_map/sub | solution.py:28
  47.2 5.4 %fusion.9 = f32[3,8,128,64]{2,3,1,0:T(8,128)} fusion(bf16[3,512,8,64]{1,3,2,0:T(8,128)(2,1)} %bitcast.85, f32[3,8,512,128]{2,3,1,0:T(8,128)} %get-tuple-element.18, f32[3,8,512]{2,1,0:T(8,128)S(1)} %get-tuple-element.17), kind=kOutput, calls=%fused_computation.16 | convolution fusion | flops 204472320 | bytes 8699904 | tf_op jit(solution)/shard_map/lhrm,lrhd->lmhd/dot_general | solution.py:56
  52.6 0.0 copy-done.4
  52.6 2.4 %copy.31 = f32[3,128,512]{2,1,0:T(8,128)} copy(f32[3,128,512]{1,2,0:T(8,128)} %bitcast.88) | data formatting | bytes 1572864 | tf_op jit(solution)/shard_map/reshape | solution.py:61
  55.1 6.8 %convolution_convert_fusion.3 = bf16[3,512,128]{2,1,0:T(8,128)(2,1)S(1)} fusion(bf16[3,512,4096]{2,1,0:T(8,128)(2,1)} %param.8, bf16[128,4096]{1,0:T(8,128)(2,1)S(1)} %copy-done.2), kind=kOutput, calls=%fused_computation.20 | convolution fusion | flops 1610809344 | bytes 14024704 | tf_op jit(solution)/shard_map/md,lcd->lmc/dot_general | solution.py:17
  61.9 0.0 slice-start.3
  62.0 3.8 %fusion.1 = (f32[3,8,512]{2,1,0:T(8,128)S(1)}, f32[3,8,128,512]{3,2,1,0:T(8,128)}) fusion(f32[3,8,512,128]{2,3,1,0:T(8,128)S(1)} %bitcast.76, f32[3,8,512]{2,1,0:T(8,128)S(1)} %get-tuple-element.17, bf16[3,128,8,64]{1,3,2,0:T(8,128)(2,1)S(1)} %bitcast.89, bf16[3,512,8,64]{1,3,2,0:T(8,128)(2,1)S(1)} %bitcast.86), kind=kOutput, calls=%fused_computation.3 | convolution fusion | flops 206032896 | bytes 14647296 | tf_op jit(solution)/shard_map/lrhd,lmhd->lhrm/dot_general | solution.py:41
  65.8 0.0 slice-done.3
  65.8 0.0 copy-start.1
  65.8 4.8 %fusion.3 = bf16[3,8,512,128]{2,3,1,0:T(8,128)(2,1)S(1)} fusion(f32[3,8,128,512]{3,2,1,0:T(8,128)} %get-tuple-element.20, f32[3,8,512]{2,1,0:T(8,128)S(1)} %get-tuple-element.19, f32[3,8,512,128]{2,3,1,0:T(8,128)S(1)} %bitcast.78, f32[3,8,512]{2,1,0:T(8,128)S(1)} %get-tuple-element.17), kind=kLoop, calls=%fused_computation.5 | loop fusion | flops 6291456 | bytes 15826944 | tf_op jit(solution)/shard_map/convert_element_type | solution.py:45
  70.7 2.1 %fusion.25 = f32[3,8,128,64]{2,3,1,0:T(8,128)} fusion(bf16[3,8,512,128]{2,3,1,0:T(8,128)(2,1)S(1)} %fusion.3, bf16[3,512,8,64]{1,3,2,0:T(8,128)(2,1)S(1)} %bitcast.80), kind=kOutput, calls=%fused_computation.33 | convolution fusion | flops 201326592 | bytes 5505024 | tf_op jit(solution)/shard_map/lhrm,lrhd->lmhd/dot_general | solution.py:53
  72.8 2.3 %copy.29 = f32[3,128,512]{2,1,0:T(8,128)} copy(f32[3,128,512]{1,2,0:T(8,128)} %bitcast.82) | data formatting | bytes 1572864 | tf_op jit(solution)/shard_map/reshape | solution.py:55
  75.0 59.6 %all-reduce.2 = (bf16[3,128,512]{2,1,0:T(8,128)(2,1)}, bf16[3,128,512]{2,1,0:T(8,128)(2,1)S(1)}) all-reduce(f32[3,128,512]{2,1,0:T(8,128)} %copy.31, f32[3,128,512]{2,1,0:T(8,128)} %copy.29), channel_id=1, replica_groups=mesh['dp'=4,'mp'=8] {'dp'}, use_global_device_ids=true, to_apply=%region_4.0 | all-reduce | flops 393216 | bytes 2359296 | tf_op jit(solution)/shard_map/psum | solution.py:62
  134.6 6.5 %convolution_bitcast_fusion = f32[128,4096]{1,0:T(8,128)S(1)} fusion(bf16[3,512,4096]{2,1,0:T(8,128)(2,1)} %param.8, bf16[3,128,512]{2,1,0:T(8,128)(2,1)} %get-tuple-element.15), kind=kOutput, calls=%fused_computation.10 | convolution fusion | flops 1610612736 | bytes 15073280 | tf_op jit(solution)/shard_map/lmc,lcd->md/dot_general | solution.py:73
  141.1 7.9 %fusion.6 = f32[128,4096]{1,0:T(8,128)} fusion(f32[128,4096]{1,0:T(8,128)S(1)} %convolution_bitcast_fusion, bf16[3,512,4096]{2,1,0:T(8,128)(2,1)} %param.7, bf16[3,128,512]{2,1,0:T(8,128)(2,1)S(1)} %get-tuple-element.16), kind=kOutput, calls=%fused_computation.12 | convolution fusion | flops 1611137024 | bytes 17170432 | tf_op jit(solution)/shard_map/lmc,lcd->md/dot_general | solution.py:72
  149.0 0.0 reduce-scatter.2.cloned.1.call-update
  149.1 4.6 %convolution_convert_fusion.1 = bf16[3,8,64,512]{3,2,1,0:T(8,128)(2,1)} fusion(bf16[3,128,8,64]{1,3,2,0:T(8,128)(2,1)} %bitcast.90, f32[3,8,512,128]{2,3,1,0:T(8,128)} %get-tuple-element.18, f32[3,8,512]{2,1,0:T(8,128)} %copy-done.7), kind=kOutput, calls=%fused_computation.15 | convolution fusion | flops 205258752 | bytes 8306688 | tf_op jit(solution)/shard_map/lhrm,lmhd->lrhd/dot_general | solution.py:32
  153.6 2.6 %copy.34 = bf16[3,512,512]{2,1,0:T(8,128)(2,1)} copy(bf16[3,512,512]{1,2,0:T(8,128)(2,1)} %bitcast.87) | data formatting | bytes 3145728
  156.2 2.7 %convolution_convert_fusion = bf16[3,8,64,512]{3,2,1,0:T(8,128)(2,1)} fusion(bf16[3,128,8,64]{1,3,2,0:T(8,128)(2,1)} %bitcast.84, bf16[3,8,512,128]{2,3,1,0:T(8,128)(2,1)S(1)} %fusion.3), kind=kOutput, calls=%fused_computation.14 | convolution fusion | flops 202113024 | bytes 5111808 | tf_op jit(solution)/shard_map/lhrm,lmhd->lrhd/dot_general | solution.py:47
  158.9 2.6 %copy.35 = bf16[3,512,512]{2,1,0:T(8,128)(2,1)} copy(bf16[3,512,512]{1,2,0:T(8,128)(2,1)} %bitcast.81) | data formatting | bytes 3145728
  161.5 12.1 %fusion.14 = f32[3,512,4096]{2,1,0:T(8,128)} fusion(bf16[128,4096]{1,0:T(8,128)(2,1)} %all-gather.2.cloned.1.call-done, bf16[3,128,512]{2,1,0:T(8,128)(2,1)S(1)} %get-tuple-element.16), kind=kOutput, calls=%fused_computation.23 | convolution fusion | flops 1610612736 | bytes 26607616 | tf_op jit(solution)/shard_map/lmc,md->lcd/dot_general | solution.py:65
  173.6 10.7 %fusion.12 = f32[3,512,4096]{2,1,0:T(8,128)} fusion(bf16[128,4096]{1,0:T(8,128)(2,1)S(1)} %copy-done.3, bf16[3,128,512]{2,1,0:T(8,128)(2,1)S(1)} %copy-done.6), kind=kOutput, calls=%fused_computation.21 | convolution fusion | flops 1610612736 | bytes 26607616 | tf_op jit(solution)/shard_map/lmc,md->lcd/dot_general | solution.py:68
  (22 shorter events, 0.0 us)
Async XLA Ops:
  7.2 27.3 %all-gather.2.cloned.1.call-start = ((), (), s32[]{:S(2)}) async-start(), calls=%async_computation.1 | async-start | bytes 1179648 | tf_op jit(solution)/shard_map/all_gather | solution.py:12
  7.9 176.4 %reduce-scatter.2.cloned.1.call-start = ((), (), s32[]{:S(2)}) async-start(), calls=%async_computation.2 | async-start | bytes 2359296 | tf_op jit(solution)/shard_map/reduce_scatter | solution.py:71
  9.7 33.0 %copy-start = (bf16[3,512,512]{1,2,0:T(8,128)(2,1)}, bf16[3,512,512]{1,2,0:T(8,128)(2,1)S(1)}, u32[]{:S(2)}) copy-start(bf16[3,512,512]{1,2,0:T(8,128)(2,1)S(1)} %copy.24) | copy-start | bytes 4718596
  42.7 9.9 %copy-start.4 = (bf16[3,512,128]{2,1,0:T(8,128)(2,1)}, bf16[3,512,128]{2,1,0:T(8,128)(2,1)S(1)}, u32[]{:S(2)}) copy-start(bf16[3,512,128]{2,1,0:T(8,128)(2,1)S(1)} %convolution_convert_fusion.2) | copy-start | bytes 1179652
  47.2 18.6 %copy-start.7 = (f32[3,8,512]{2,1,0:T(8,128)}, f32[3,8,512]{2,1,0:T(8,128)S(1)}, u32[]{:S(2)}) copy-start(f32[3,8,512]{2,1,0:T(8,128)S(1)} %get-tuple-element.17) | copy-start | bytes 147460
  47.2 7.9 %copy-start.2 = (bf16[128,4096]{1,0:T(8,128)(2,1)S(1)}, bf16[128,4096]{1,0:T(8,128)(2,1)}, u32[]{:S(2)}) copy-start(bf16[128,4096]{1,0:T(8,128)(2,1)} %all-gather.2.cloned.1.call-done) | copy-start | bytes 3145732
  52.6 9.3 %slice-start = ((s8[6291456]{0:T(1024)(128)(4,1)}), s8[2097152]{0:T(1024)(128)(4,1)S(1)}, s32[]{:S(2)}) async-start(s8[6291456]{0:T(1024)(128)(4,1)} %bitcast.75), calls=%async_computation.3 | async-start | bytes 4194304
  55.1 6.9 %slice-start.1 = ((s8[6291456]{0:T(1024)(128)(4,1)}), s8[4194304]{0:T(1024)(128)(4,1)S(1)}, s32[]{:S(2)}) async-start(s8[6291456]{0:T(1024)(128)(4,1)} %bitcast.75), calls=%async_computation.4 | async-start | bytes 8388608
  55.1 6.9 %copy-start.5 = (bf16[3,512,512]{1,2,0:T(8,128)(2,1)S(1)}, bf16[3,512,512]{1,2,0:T(8,128)(2,1)}, u32[]{:S(2)}) copy-start(bf16[3,512,512]{1,2,0:T(8,128)(2,1)} %copy.26) | copy-start | bytes 4718596
  55.1 10.7 %slice-start.2 = ((s8[6291456]{0:T(1024)(128)(4,1)}), s8[4194304]{0:T(1024)(128)(4,1)S(1)}, s32[]{:S(2)}) async-start(s8[6291456]{0:T(1024)(128)(4,1)} %bitcast.77), calls=%async_computation.5 | async-start | bytes 8388608
  61.9 3.9 %copy-start.8 = (bf16[3,512,128]{2,1,0:T(8,128)(2,1)}, bf16[3,512,128]{2,1,0:T(8,128)(2,1)S(1)}, u32[]{:S(2)}) copy-start(bf16[3,512,128]{2,1,0:T(8,128)(2,1)S(1)} %convolution_convert_fusion.3) | copy-start | bytes 1179652
  61.9 3.9 %slice-start.3 = ((s8[6291456]{0:T(1024)(128)(4,1)}), s8[2097152]{0:T(1024)(128)(4,1)S(1)}, s32[]{:S(2)}) async-start(s8[6291456]{0:T(1024)(128)(4,1)} %bitcast.77), calls=%async_computation.6 | async-start | bytes 4194304
  65.8 4.8 %copy-start.1 = (bf16[3,512,512]{1,2,0:T(8,128)(2,1)S(1)}, bf16[3,512,512]{1,2,0:T(8,128)(2,1)}, u32[]{:S(2)}) copy-start(bf16[3,512,512]{1,2,0:T(8,128)(2,1)} %copy-done) | copy-start | bytes 4718596
  161.5 12.1 %copy-start.3 = (bf16[128,4096]{1,0:T(8,128)(2,1)S(1)}, bf16[128,4096]{1,0:T(8,128)(2,1)}, u32[]{:S(2)}) copy-start(bf16[128,4096]{1,0:T(8,128)(2,1)} %all-gather.2.cloned.1.call-done) | copy-start | bytes 3145732
  161.5 12.1 %copy-start.6 = (bf16[3,128,512]{2,1,0:T(8,128)(2,1)S(1)}, bf16[3,128,512]{2,1,0:T(8,128)(2,1)}, u32[]{:S(2)}) copy-start(bf16[3,128,512]{2,1,0:T(8,128)(2,1)} %get-tuple-element.15) | copy-start | bytes 1179652
Sparse Core Ops, SparseCore 0:
  9.6 24.7 all-gather.1
  149.2 34.6 reduce-scatter.1
where the time goes:
time: 192 us; the launch traced here: 191 us
  matrix products  75.4 us (39%)
  blocking collectives  59.6 us (31%)
  waiting for transfers between devices  22.3 us (12%)
  local copies, waits for them, and re-layouts  14.8 us (8%)
  between operations  14.2 us (7%)
  other arithmetic  4.82 us (3%)
    psum x1, blocking collectives, shards(): key_sum, value_sum = lax.psum((key_part, value_part), 'dp')  59.6 us
    all_gather x1, waiting for transfers between devices, shards(): mem_all = lax.all_gather(memory, 'mp', axis=0, tiled=True)  21.6 us
    dot_general x1, matrix products, shards(): jnp.einsum('lmc,md->lcd', key_gradient, mem_all, preferred_element_type=j...  12.1 us
    dot_general x1, matrix products, shards(): jnp.einsum('lmc,md->lcd', value_gradient, mem_all, preferred_element_type...  10.7 us
    unnamed x30, local copies, waits for them, and re-layouts  10.1 us
    dot_general x1, matrix products, shards(): jnp.einsum('md,lcd->lmc', mem_all, w_key, preferred_element_type=jnp.floa...  8.26 us
    dot_general x1, matrix products, shards(): jnp.einsum('lmc,lcd->md', key_gradient, w_key, preferred_element_type=jnp...  7.88 us
    dot_general x1, matrix products, shards(): jnp.einsum('md,lcd->lmc', mem_all, w_value, preferred_element_type=jnp.fl...  6.82 us
  transfers between devices with their start and end apart: 2, of which 1 were waited for; matrix products, arithmetic and copies ran while one was open for 21% of the time, Pallas kernels for 0%

commit v1 on v0

--- a/solution.py
+++ b/solution.py
@@ -1,9 +1,389 @@
 import jax
 import jax.numpy as jnp
 from jax import lax
+from jax.experimental import pallas as pl
+from jax.experimental.pallas import tpu as pltpu
 from jax.sharding import PartitionSpec as P
 
 HEAD_WIDTH = 64
+PAIR = 2 * HEAD_WIDTH
+MESH = pl.DeviceIdType.MESH
+F32 = jnp.float32
+BF16 = jnp.bfloat16
+
+DP, CHIPS, CORES = 4, 4, 2
+
+
+def attention_kernel(
+    q_hbm, mem_ref, wk_hbm, wv_hbm, g_hbm,
+    att_hbm, gq_hbm, kvg_hbm, mem_hbm, gm_hbm,
+    q_v, g_v, att_v, gq_v, w_v, mg, acc, kvt, part, own, landed, kvg, gm_v,
+    in_sem, w_sem, out_sem, z_send, z_recv, d_send, d_recv, s_send, s_recv,
+    rs_send, rs_recv, ag_send, ag_recv,
+):
+    layers, rows, width = q_v.shape
+    tokens = mem_ref.shape[0]
+    quarter = mem_ref.shape[1] // DP
+    mem_total = tokens * CHIPS * CORES
+    i = lax.axis_index("dp")
+    me = lax.axis_index("mp")
+    z = me // CORES
+    core = me % CORES
+    sibling = z * CORES + 1 - core
+
+    def z_peer(k):
+        return {"dp": i, "mp": ((z + k) % CHIPS) * CORES + core}
+
+    def d_peer(k):
+        return {"dp": (i + k) % DP, "mp": me}
+
+    sib = {"dp": i, "mp": sibling}
+
+    def load_w(step):
+        j = (i + DP - step) % DP
+        cols = pl.ds(pl.multiple_of(j * quarter, quarter), quarter)
+        return [
+            pltpu.make_async_copy(
+                hbm.at[:, :, cols], w_v.at[:, kv, :, cols], w_sem.at[step, kv]
+            )
+            for kv, hbm in enumerate((wk_hbm, wv_hbm))
+        ]
+
+    for step in range(DP):
+        for copy in load_w(step):
+            copy.start()
+        if step == 0:
+            load_q = pltpu.make_async_copy(q_hbm, q_v, in_sem.at[0])
+            load_g = pltpu.make_async_copy(g_hbm, g_v, in_sem.at[1])
+    load_q.start()
+    load_g.start()
+
+    barrier = pltpu.get_barrier_semaphore()
+    for k in range(1, CHIPS):
+        pl.semaphore_signal(barrier, inc=1, device_id=z_peer(k), device_id_type=MESH)
+    for k in range(1, DP):
+        pl.semaphore_signal(barrier, inc=1, device_id=d_peer(k), device_id_type=MESH)
+    pl.semaphore_signal(barrier, inc=1, device_id=sib, device_id_type=MESH)
+    pl.semaphore_wait(barrier, CHIPS + DP - 1)
+
+    mine = pl.ds(pl.multiple_of(i * quarter, quarter), quarter)
+    z_copies = []
+    for k in range(1, CHIPS):
+        z_copies.append(
+            pltpu.make_async_remote_copy(
+                src_ref=mem_ref.at[:, mine],
+                dst_ref=mg.at[i, core, z],
+                send_sem=z_send.at[k - 1],
+                recv_sem=z_recv.at[k - 1],
+                device_id=z_peer(k),
+                device_id_type=MESH,
+            )
+        )
+        z_copies[-1].start()
+    mg[i, core, z] = mem_ref[:, mine]
+    for copy in z_copies:
+        copy.wait_recv()
+
+    def to_sibling(step):
+        j = (i + DP - step) % DP
+        return pltpu.make_async_remote_copy(
+            src_ref=mg.at[j, core],
+            dst_ref=mg.at[j, core],
+            send_sem=s_send.at[step],
+            recv_sem=s_recv.at[step],
+            device_id=sib,
+            device_id_type=MESH,
+        )
+
+    d_copies = []
+    s_copies = [to_sibling(0)]
+    s_copies[0].start()
+    for k in range(1, DP):
+        d_copies.append(
+            pltpu.make_async_remote_copy(
+                src_ref=mg.at[i, core],
+                dst_ref=mg.at[i, core],
+                send_sem=d_send.at[k - 1],
+                recv_sem=d_recv.at[k - 1],
+                device_id=d_peer(k),
+                device_id_type=MESH,
+            )
+        )
+        d_copies[-1].start()
+
+    acc[...] = jnp.zeros_like(acc)
+    for step in range(DP):
+        j = (i + DP - step) % DP
+        cols = pl.ds(pl.multiple_of(j * quarter, quarter), quarter)
+        if step >= 1:
+            d_copies[step - 1].wait_recv()
+            s_copies.append(to_sibling(step))
+            s_copies[step].start()
+        for copy in load_w(step):
+            copy.wait()
+        s_copies[step].wait_recv()
+
+        @pl.loop(0, layers * 2)
+        def project(n):
+            mem_cols = mg[j].reshape(mem_total, quarter)
+            acc[n // 2, n % 2] += lax.dot_general(
+                w_v[n // 2, n % 2, :, cols],
+                mem_cols,
+                (((1,), (1,)), ((), ())),
+                preferred_element_type=F32,
+            )
+
+    kvt[...] = acc[...].astype(BF16)
+    for copy in z_copies + d_copies + s_copies:
+        copy.wait_send()
+    mem_out = pltpu.make_async_copy(mg, mem_hbm, out_sem.at[0])
+    mem_out.start()
+    load_q.wait()
+    load_g.wait()
+
+    def pair_rows(pair):
+        return pl.ds(pl.multiple_of(pair * PAIR, PAIR), PAIR)
+
+    def rs_copy(layer, t):
+        return pltpu.make_async_remote_copy(
+            src_ref=part.at[layer, t],
+            dst_ref=landed.at[layer, t],
+            send_sem=rs_send.at[layer, t],
+            recv_sem=rs_recv.at[layer, t],
+            device_id={"dp": (i + 1 + t) % DP, "mp": me},
+            device_id_type=MESH,
+        )
+
+    def ag_copy(layer, k):
+        block = kvg.at[layer, :, pair_rows(i), :]
+        return pltpu.make_async_remote_copy(
+            src_ref=block,
+            dst_ref=block,
+            send_sem=ag_send.at[layer, k - 1],
+            recv_sem=ag_recv.at[layer, k - 1],
+            device_id=d_peer(k),
+            device_id_type=MESH,
+        )
+
+    def reduce(layer):
+        total = own[layer]
+        for t in range(DP - 1):
+            rs_copy(layer, t).wait_recv()
+            total = total + landed[layer, t].astype(F32)
+        kvg[layer, :, pair_rows(i), :] = total.astype(BF16)
+        for k in range(1, DP):
+            ag_copy(layer, k).start()
+
+    first_head = lax.broadcasted_iota(jnp.int32, (PAIR, mem_total), 0) < HEAD_WIDTH
+
+    def block_diagonal(block):
+        zero = jnp.zeros_like(block)
+        return jnp.concatenate(
+            [jnp.where(first_head, block, zero), jnp.where(first_head, zero, block)], axis=1
+        )
+
+    def own_blocks(both):
+        return jnp.where(first_head, both[:, :mem_total], both[:, mem_total:])
+
+    @pl.loop(0, layers * DP)
+    def attend(n):
+        layer = n // DP
+        t = n % DP
+        pair = (i + 1 + t) % DP
+        lanes = pair_rows(pair)
+        queries = q_v[layer, :, lanes]
+        grads = g_v[layer, :, lanes]
+        keys = block_diagonal(kvt[layer, 0, lanes, :])
+        values = block_diagonal(kvt[layer, 1, lanes, :])
+        scores = jnp.dot(queries, keys, preferred_element_type=F32)
+        grad_probs = jnp.dot(grads, values, preferred_element_type=F32)
+        probs_b, grad_scores = [], []
+        for head in range(2):
+            at = slice(head * mem_total, (head + 1) * mem_total)
+            s = scores[:, at]
+            gp = grad_probs[:, at]
+            e = jnp.exp(s - jnp.max(s, axis=-1, keepdims=True))
+            probs = e * (1.0 / jnp.sum(e, axis=-1, keepdims=True))
+            delta = jnp.sum(probs * gp, axis=-1, keepdims=True)
+            probs_b.append(probs.astype(BF16))
+            grad_scores.append((probs * (gp - delta)).astype(BF16))
+        probs_b = jnp.concatenate(probs_b, axis=1)
+        grad_scores = jnp.concatenate(grad_scores, axis=1)
+        nt = (((1,), (1,)), ((), ()))
+        tn = (((0,), (0,)), ((), ()))
+        att_v[layer, :, lanes] = lax.dot_general(
+            probs_b, values, nt, preferred_element_type=F32
+        ).astype(BF16)
+        gq_v[layer, :, lanes] = lax.dot_general(
+            grad_scores, keys, nt, preferred_element_type=F32
+        ).astype(BF16)
+        grad_keys = own_blocks(
+            lax.dot_general(queries, grad_scores, tn, preferred_element_type=F32)
+        )
+        grad_values = own_blocks(
+            lax.dot_general(grads, probs_b, tn, preferred_element_type=F32)
+        )
+
+        @pl.when(t < DP - 1)
+        def _():
+            part[layer, t, 0] = grad_keys.astype(BF16)
+            part[layer, t, 1] = grad_values.astype(BF16)
+            rs_copy(layer, t).start()
+
+        @pl.when(t == DP - 1)
+        def _():
+            own[layer, 0] = grad_keys
+            own[layer, 1] = grad_values
+
+        @pl.when((t == 1) & (layer >= 1))
+        def _():
+            reduce(layer - 1)
+
+    att_out = pltpu.make_async_copy(att_v, att_hbm, out_sem.at[1])
+    gq_out = pltpu.make_async_copy(gq_v, gq_hbm, out_sem.at[2])
+    att_out.start()
+    gq_out.start()
+    reduce(layers - 1)
+
+    for layer in range(layers):
+        for k in range(1, DP):
+            ag_copy(layer, k).wait_recv()
+        for kv in range(2):
+            term = lax.dot_general(
+                kvg[layer, kv],
+                w_v[layer, kv, :, mine],
+                (((0,), (0,)), ((), ())),
+                preferred_element_type=F32,
+            )
+            if layer == 0 and kv == 0:
+                gm_v[...] = term
+            else:
+                gm_v[...] += term
+    for layer in range(layers):
+        for t in range(DP - 1):
+            rs_copy(layer, t).wait_send()
+            ag_copy(layer, t + 1).wait_send()
+    kvg_out = pltpu.make_async_copy(kvg, kvg_hbm, out_sem.at[3])
+    gm_out = pltpu.make_async_copy(gm_v, gm_hbm, out_sem.at[4])
+    kvg_out.start()
+    gm_out.start()
+    for copy in (mem_out, att_out, gq_out, kvg_out, gm_out):
+        copy.wait()
+
+
+def attention(queries, memory, w_key, w_value, grad_out):
+    layers, rows, width = queries.shape
+    tokens, model = memory.shape
+    quarter = model // DP
+    mem_total = tokens * CHIPS * CORES
+    any_spec = pl.BlockSpec(memory_space=pl.ANY)
+    dma = pltpu.SemaphoreType.DMA
+    out_shape = (
+        jax.ShapeDtypeStruct(queries.shape, BF16),
+        jax.ShapeDtypeStruct(queries.shape, BF16),
+        jax.ShapeDtypeStruct((layers, 2, width, mem_total), BF16),
+        jax.ShapeDtypeStruct((DP, CORES, CHIPS, tokens, quarter), BF16),
+        jax.ShapeDtypeStruct((mem_total, quarter), F32),
+    )
+    return pl.pallas_call(
+        attention_kernel,
+        out_shape=out_shape,
+        in_specs=[
+            any_spec,
+            pl.BlockSpec(memory_space=pltpu.VMEM),
+            any_spec,
+            any_spec,
+            any_spec,
+        ],
+        out_specs=(any_spec,) * 5,
+        scratch_shapes=[
+            pltpu.VMEM(queries.shape, BF16),
+            pltpu.VMEM(queries.shape, BF16),
+            pltpu.VMEM(queries.shape, BF16),
+            pltpu.VMEM(queries.shape, BF16),
+            pltpu.VMEM((layers, 2, width, model), BF16),
+            pltpu.VMEM((DP, CORES, CHIPS, tokens, quarter), BF16),
+            pltpu.VMEM((layers, 2, width, mem_total), F32),
+            pltpu.VMEM((layers, 2, width, mem_total), BF16),
+            pltpu.VMEM((layers, DP - 1, 2, PAIR, mem_total), BF16),
+            pltpu.VMEM((layers, 2, PAIR, mem_total), F32),
+            pltpu.VMEM((layers, DP - 1, 2, PAIR, mem_total), BF16),
+            pltpu.VMEM((layers, 2, width, mem_total), BF16),
+            pltpu.VMEM((mem_total, quarter), F32),
+            dma((2,)),
+            dma((DP, 2)),
+            dma((5,)),
+            dma((CHIPS - 1,)),
+            dma((CHIPS - 1,)),
+            dma((DP - 1,)),
+            dma((DP - 1,)),
+            dma((DP,)),
+            dma((DP,)),
+            dma((layers, DP - 1)),
+            dma((layers, DP - 1)),
+            dma((layers, DP - 1)),
+            dma((layers, DP - 1)),
+        ],
+        compiler_params=pltpu.CompilerParams(
+            collective_id=0, has_side_effects=True, vmem_limit_bytes=52 * 2**20
+        ),
+        cost_estimate=pl.CostEstimate(
+            flops=8 * 10**9, bytes_accessed=35 * 10**6, transcendentals=2 * 10**6
+        ),
+        name="attention",
+    )(queries, memory, w_key, w_value, grad_out)
+
+
+def weight_kernel(kvg_ref, mem_ref, gwk_ref, gwv_ref):
+    quarter = mem_ref.shape[-1]
+    for kv, out in enumerate((gwk_ref, gwv_ref)):
+        for j in range(DP):
+            out[0, :, j * quarter : (j + 1) * quarter] = jnp.dot(
+                kvg_ref[0, kv], mem_ref[j], preferred_element_type=F32
+            )
+
+
+def weight_gradients(kvg, mem):
+    layers, _, width, mem_total = kvg.shape
+    quarter = mem.shape[-1]
+    model = DP * quarter
+    rows = 128
+    out = jax.ShapeDtypeStruct((layers, width, model), F32)
+    return pl.pallas_call(
+        weight_kernel,
+        grid=(layers, width // rows),
+        in_specs=[
+            pl.BlockSpec((1, 2, rows, mem_total), lambda l, c: (l, 0, c, 0)),
+            pl.BlockSpec((DP, mem_total, quarter), lambda l, c: (0, 0, 0)),
+        ],
+        out_specs=[pl.BlockSpec((1, rows, model), lambda l, c: (l, c, 0))] * 2,
+        out_shape=(out, out),
+        compiler_params=pltpu.CompilerParams(vmem_limit_bytes=32 * 2**20),
+        cost_estimate=pl.CostEstimate(
+            flops=4 * layers * width * mem_total * model,
+            bytes_accessed=8 * layers * width * model,
+            transcendentals=0,
+        ),
+        name="weight_gradients",
+    )(kvg, mem)
+
+
+def fused_shards(queries, memory, w_key, w_value, grad_out):
+    attended, grad_queries, kvg, mem, gm_part = attention(
+        queries, memory, w_key, w_value, grad_out
+    )
+    tokens = memory.shape[0]
+    mem_total = tokens * CHIPS * CORES
+    quarter = mem.shape[-1]
+    gm_part = (
+        gm_part.reshape(CORES, CHIPS, tokens, quarter)
+        .transpose(1, 0, 2, 3)
+        .reshape(mem_total, quarter)
+    )
+    gm = lax.psum_scatter(gm_part, "mp", scatter_dimension=0, tiled=True)
+    grad_memory = lax.all_gather(gm, "dp", axis=1, tiled=True)
+    grad_w_key, grad_w_value = weight_gradients(kvg, mem.reshape(DP, mem_total, quarter))
+    return attended, grad_queries, grad_memory, grad_w_key, grad_w_value
 
 
 def shards(queries, memory, w_key, w_value, grad_out):
@@ -79,8 +459,19 @@
 
 
 def solution(mesh):
+    def choose(queries, memory, w_key, w_value, grad_out):
+        fits = (
+            mesh.shape["dp"] == DP
+            and mesh.shape["mp"] == CHIPS * CORES
+            and queries.shape[2] == DP * PAIR
+            and memory.shape[0] == 16
+            and memory.shape[1] % (DP * 128) == 0
+        )
+        run = fused_shards if fits else shards
+        return run(queries, memory, w_key, w_value, grad_out)
+
     return jax.shard_map(
-        shards,
+        choose,
         mesh=mesh,
         in_specs=(
             P(None, "dp", "mp"),

time: 192 us -> 110 us (0.57)
  matrix products: 75.4 us -> 0 us
  Pallas kernels: 0 us -> 66 us
  blocking collectives: 59.6 us -> 9.16 us
  local copies, waits for them, and re-layouts: 14.8 us -> 6.1 us
  waiting for transfers between devices: 22.3 us -> 13.9 us
  other arithmetic: 4.82 us -> 0 us
    dot_general x11 -> x0, matrix products: 70.9 us -> none  [the longest x1 12.1 us: shards(): jnp.einsum('lmc,md->lcd', key_gradient, mem_all, preferred_element_type=j...]
    pallas_call x0 -> x2, Pallas kernels: none -> 66 us  [the longest x1 49.5 us: attention(): pl.pallas_call(attention_kernel, out_shape=out_shape, in_specs=[any_spec,...]
    psum x1 -> x0, blocking collectives: 59.6 us -> none  [shards(): key_sum, value_sum = lax.psum((key_part, value_part), 'dp')]
    all_gather x1 -> x0, waiting for transfers between devices: 21.6 us -> none  [shards(): mem_all = lax.all_gather(memory, 'mp', axis=0, tiled=True)]
    reduce_scatter x1, waiting for transfers between devices: 0.01 us -> 13.9 us  [fused_shards(): gm = lax.psum_scatter(gm_part, 'mp', scatter_dimension=0, tiled=True)]
    all_gather x0 -> x1, blocking collectives: none -> 9.16 us  [fused_shards(): grad_memory = lax.all_gather(gm, 'dp', axis=1, tiled=True)]
    unnamed x30 -> x11, local copies, waits for them, and re-layouts: 10.1 us -> 5.25 us
    convert_element_type x1 -> x0, other arithmetic: 4.82 us -> none  [shards(): (attn_probs * (probability_gradient - row_delta)).astype(jnp.bfloat16)]
  transfers between devices with their start and end apart: 2 -> 1, of which waited for: 1 -> 1; matrix products, arithmetic and copies ran while one was open for 21% -> 0% of each run, Pallas kernels for 0% -> 15%
where the time goes in v1:
time: 110 us; the launch traced here: 109 us
  Pallas kernels  66 us (60%)
  between operations  14.1 us (13%)
  waiting for transfers between devices  13.9 us (13%)
  blocking collectives  9.16 us (8%)
  local copies, waits for them, and re-layouts  6.1 us (6%)
    pallas_call x1, Pallas kernels, attention(): pl.pallas_call(attention_kernel, out_shape=out_shape, in_specs=[any_spec,...  49.5 us
    pallas_call x1, Pallas kernels, weight_gradients(): pl.pallas_call(weight_kernel, grid=(layers, width // rows), in_specs=[pl....  16.5 us
    reduce_scatter x1, waiting for transfers between devices, fused_shards(): gm = lax.psum_scatter(gm_part, 'mp', scatter_dimension=0, tiled=True)  13.9 us
    all_gather x1, blocking collectives, fused_shards(): grad_memory = lax.all_gather(gm, 'dp', axis=1, tiled=True)  9.16 us
    unnamed x11, local copies, waits for them, and re-layouts  5.25 us
  transfers between devices with their start and end apart: 1, of which 1 were waited for; matrix products, arithmetic and copies ran while one was open for 0% of the time, Pallas kernels for 15%

profile of v1, /device:TPU:0, one launch (start us, length us, event | category | flops | bytes accessed | tf_op | source)
XLA Modules:
  0.0 109.3 jit_solution(7296431905721454908)
XLA Ops:
  7.2 0.0 reduce-scatter.2.cloned.1.call-start
  7.2 0.0 copy-start
  7.2 0.9 copy-done
  8.1 49.5 %attention.1 = (bf16[3,512,512]{2,1,0:T(8,128)(2,1)}, bf16[3,512,512]{2,1,0:T(8,128)(2,1)}, bf16[3,2,512,128]{3,2,1,0:T(8,128)(2,1)S(1)}, bf16[4,2,4,16,1024]{4,3,2,1,0:T(8,128)(2,1)}, f32[128,1024]{1,0:T(8,128)S(1)}) custom-call(bf16[3,512,512]{2,1,0:T(8,128)(2,1)} %q_hbm.1, bf16[16,4096]{1,0:T(8,128)(2,1)S(1)} %copy-done, bf16[3,512,4096]{2,1,0:T(8,128)(2,1)} %wk_hbm.1, ...), custom_call_target="tpu_custom_call" | custom-call | flops 8000000000 | bytes 35000000 | tf_op jit(solution)/shard_map/attention/pallas_call | solution.py:288
  57.6 0.0 copy-start.1
  57.6 0.8 copy.10
  58.5 0.0 reduce-scatter.2.cloned.1.call-update
  58.5 0.5 copy-done.1
  59.0 0.0 copy-start.3
  59.0 16.5 %weight_gradients.1 = (f32[3,512,4096]{2,1,0:T(8,128)}, f32[3,512,4096]{2,1,0:T(8,128)}) custom-call(bf16[3,2,512,128]{3,2,1,0:T(8,128)(2,1)S(1)} %get-tuple-element.15.kvg_ref, bf16[4,128,1024]{2,1,0:T(8,128)(2,1)S(1)} %bitcast.6), custom_call_target="tpu_custom_call" | custom-call | flops 3221225472 | bytes 50331648 | tf_op jit(solution)/shard_map/weight_gradients/pallas_call | solution.py:352
  75.5 13.9 %reduce-scatter.2.cloned.1.call-done = f32[16,1024]{1,0:T(8,128)} async-done(((f32[128,1024]{1,0:T(8,128)}), f32[16,1024]{1,0:T(8,128)}) %reduce-scatter.2.cloned.1.call-update) | async-done | bytes 65552 | tf_op jit(solution)/shard_map/reduce_scatter | solution.py:383
  89.4 9.2 %all_gather.3 = f32[16,4096]{1,0:T(8,128)S(1)} all-gather(f32[16,1024]{1,0:T(8,128)} %reduce-scatter.2.cloned.1.call-done), channel_id=1, replica_groups=mesh['dp'=4,'mp'=8] {'dp'}, dimensions={1}, use_global_device_ids=true | all-gather | bytes 327680 | tf_op jit(solution)/shard_map/all_gather | solution.py:384
  98.6 0.0 copy-done.3
  98.6 0.0 copy-start.2
  98.6 1.1 %copy.14 = bf16[3,512,512]{2,1,0:T(8,128)(2,1)} copy(bf16[3,512,512]{2,1,0:T(8,128)(2,1)S(1)} %copy-done.3) | data formatting | bytes 3145728
  99.7 0.8 copy-done.2
  100.6 1.1 %copy.15 = bf16[3,512,512]{2,1,0:T(8,128)(2,1)} copy(bf16[3,512,512]{2,1,0:T(8,128)(2,1)S(1)} %copy-done.2) | data formatting | bytes 3145728
  101.7 0.7 copy.16
Async XLA Ops:
  7.2 82.3 %reduce-scatter.2.cloned.1.call-start = ((), (), s32[]{:S(2)}) async-start(), calls=%async_computation.1 | async-start | bytes 589824 | tf_op jit(solution)/shard_map/reduce_scatter | solution.py:383
  7.2 0.9 copy-start
  57.6 1.4 %copy-start.1 = (bf16[4,2,4,16,1024]{4,3,2,1,0:T(8,128)(2,1)S(1)}, bf16[4,2,4,16,1024]{4,3,2,1,0:T(8,128)(2,1)}, u32[]{:S(2)}) copy-start(bf16[4,2,4,16,1024]{4,3,2,1,0:T(8,128)(2,1)} %get-tuple-element.16) | copy-start | bytes 3145732
  59.0 39.6 %copy-start.3 = (bf16[3,512,512]{2,1,0:T(8,128)(2,1)S(1)}, bf16[3,512,512]{2,1,0:T(8,128)(2,1)}, u32[]{:S(2)}) copy-start(bf16[3,512,512]{2,1,0:T(8,128)(2,1)} %get-tuple-element.24) | copy-start | bytes 4718596
  98.6 2.0 %copy-start.2 = (bf16[3,512,512]{2,1,0:T(8,128)(2,1)S(1)}, bf16[3,512,512]{2,1,0:T(8,128)(2,1)}, u32[]{:S(2)}) copy-start(bf16[3,512,512]{2,1,0:T(8,128)(2,1)} %get-tuple-element.25) | copy-start | bytes 4718596
Sparse Core Ops, SparseCore 0:
  58.6 30.7 reduce-scatter.1

commit v2 on v1

--- a/solution.py
+++ b/solution.py
@@ -15,11 +15,12 @@
 
 
 def attention_kernel(
-    q_hbm, mem_ref, wk_hbm, wv_hbm, g_hbm,
-    att_hbm, gq_hbm, kvg_hbm, mem_hbm, gm_hbm,
-    q_v, g_v, att_v, gq_v, w_v, mg, acc, kvt, part, own, landed, kvg, gm_v,
+    q_hbm, mem_in, wk_hbm, wv_hbm, g_hbm,
+    att_hbm, gq_hbm, kvg_hbm, mem_hbm, gm0_hbm, gm1_hbm, gm2_hbm, gm3_hbm,
+    q_v, g_v, qt_v, gt_v, att_v, gq_v, w_v, mem_ref, mg, acc, kvt, part, own, landed, kvg,
+    gm_v, gm_landed,
     in_sem, w_sem, out_sem, z_send, z_recv, d_send, d_recv, s_send, s_recv,
-    rs_send, rs_recv, ag_send, ag_recv,
+    rs_send, rs_recv, ag_send, ag_recv, gm_sem,
 ):
     layers, rows, width = q_v.shape
     tokens = mem_ref.shape[0]
@@ -49,14 +50,15 @@
             for kv, hbm in enumerate((wk_hbm, wv_hbm))
         ]
 
+    load_mem = pltpu.make_async_copy(mem_in, mem_ref, in_sem.at[2])
+    load_q = pltpu.make_async_copy(q_hbm, q_v, in_sem.at[0])
+    load_g = pltpu.make_async_copy(g_hbm, g_v, in_sem.at[1])
+    load_mem.start()
+    load_q.start()
+    load_g.start()
     for step in range(DP):
         for copy in load_w(step):
             copy.start()
-        if step == 0:
-            load_q = pltpu.make_async_copy(q_hbm, q_v, in_sem.at[0])
-            load_g = pltpu.make_async_copy(g_hbm, g_v, in_sem.at[1])
-    load_q.start()
-    load_g.start()
 
     barrier = pltpu.get_barrier_semaphore()
     for k in range(1, CHIPS):
@@ -64,6 +66,7 @@
     for k in range(1, DP):
         pl.semaphore_signal(barrier, inc=1, device_id=d_peer(k), device_id_type=MESH)
     pl.semaphore_signal(barrier, inc=1, device_id=sib, device_id_type=MESH)
+    load_mem.wait()
     pl.semaphore_wait(barrier, CHIPS + DP - 1)
 
     mine = pl.ds(pl.multiple_of(i * quarter, quarter), quarter)
@@ -111,6 +114,18 @@
         )
         d_copies[-1].start()
 
+    def pair_rows(pair):
+        return pl.ds(pl.multiple_of(pair * PAIR, PAIR), PAIR)
+
+    load_q.wait()
+    load_g.wait()
+
+    @pl.loop(0, layers * DP)
+    def turn(n):
+        lanes = pair_rows(n % DP)
+        qt_v[n // DP, lanes, :] = q_v[n // DP, :, lanes].T
+        gt_v[n // DP, lanes, :] = g_v[n // DP, :, lanes].T
+
     acc[...] = jnp.zeros_like(acc)
     for step in range(DP):
         j = (i + DP - step) % DP
@@ -138,11 +153,6 @@
         copy.wait_send()
     mem_out = pltpu.make_async_copy(mg, mem_hbm, out_sem.at[0])
     mem_out.start()
-    load_q.wait()
-    load_g.wait()
-
-    def pair_rows(pair):
-        return pl.ds(pl.multiple_of(pair * PAIR, PAIR), PAIR)
 
     def rs_copy(layer, t):
         return pltpu.make_async_remote_copy(
@@ -185,10 +195,7 @@
     def own_blocks(both):
         return jnp.where(first_head, both[:, :mem_total], both[:, mem_total:])
 
-    @pl.loop(0, layers * DP)
-    def attend(n):
-        layer = n // DP
-        t = n % DP
+    def attend(layer, t):
         pair = (i + 1 + t) % DP
         lanes = pair_rows(pair)
         queries = q_v[layer, :, lanes]
@@ -210,7 +217,6 @@
         probs_b = jnp.concatenate(probs_b, axis=1)
         grad_scores = jnp.concatenate(grad_scores, axis=1)
         nt = (((1,), (1,)), ((), ()))
-        tn = (((0,), (0,)), ((), ()))
         att_v[layer, :, lanes] = lax.dot_general(
             probs_b, values, nt, preferred_element_type=F32
         ).astype(BF16)
@@ -218,34 +224,39 @@
             grad_scores, keys, nt, preferred_element_type=F32
         ).astype(BF16)
         grad_keys = own_blocks(
-            lax.dot_general(queries, grad_scores, tn, preferred_element_type=F32)
+            jnp.dot(qt_v[layer, lanes, :], grad_scores, preferred_element_type=F32)
         )
         grad_values = own_blocks(
-            lax.dot_general(grads, probs_b, tn, preferred_element_type=F32)
-        )
-
-        @pl.when(t < DP - 1)
-        def _():
-            part[layer, t, 0] = grad_keys.astype(BF16)
-            part[layer, t, 1] = grad_values.astype(BF16)
-            rs_copy(layer, t).start()
-
-        @pl.when(t == DP - 1)
-        def _():
-            own[layer, 0] = grad_keys
-            own[layer, 1] = grad_values
-
-        @pl.when((t == 1) & (layer >= 1))
+            jnp.dot(gt_v[layer, lanes, :], probs_b, preferred_element_type=F32)
+        )
+        return grad_keys, grad_values
+
+    def send_part(layer, t, grads):
+        for kv in range(2):
+            part[layer, t, kv] = grads[kv].astype(BF16)
+        rs_copy(layer, t).start()
+
+    @pl.loop(0, layers)
+    def one_layer(layer):
+        first, second = attend(layer, 0), attend(layer, 1)
+        send_part(layer, 0, first)
+        send_part(layer, 1, second)
+
+        @pl.when(layer >= 1)
         def _():
             reduce(layer - 1)
+
+        third, last = attend(layer, 2), attend(layer, 3)
+        send_part(layer, 2, third)
+        for kv in range(2):
+            own[layer, kv] = last[kv]
 
     att_out = pltpu.make_async_copy(att_v, att_hbm, out_sem.at[1])
     gq_out = pltpu.make_async_copy(gq_v, gq_hbm, out_sem.at[2])
     att_out.start()
     gq_out.start()
-    reduce(layers - 1)
-
-    for layer in range(layers):
+
+    def add_memory_gradient(layer):
         for k in range(1, DP):
             ag_copy(layer, k).wait_recv()
         for kv in range(2):
@@ -254,20 +265,43 @@
                 w_v[layer, kv, :, mine],
                 (((0,), (0,)), ((), ())),
                 preferred_element_type=F32,
-            )
+            ).reshape(CORES, CHIPS, tokens, quarter)
             if layer == 0 and kv == 0:
                 gm_v[...] = term
             else:
                 gm_v[...] += term
+
+    for layer in range(layers):
+        if layer == layers - 1:
+            reduce(layer)
+            add_memory_gradient(layer - 1)
+            add_memory_gradient(layer)
+        elif layer < layers - 2:
+            add_memory_gradient(layer)
+    kvg_out = pltpu.make_async_copy(kvg, kvg_hbm, out_sem.at[3])
+    kvg_out.start()
+    gm_copy = pltpu.make_async_remote_copy(
+        src_ref=gm_v.at[1 - core],
+        dst_ref=gm_landed,
+        send_sem=gm_sem.at[0],
+        recv_sem=gm_sem.at[1],
+        device_id=sib,
+        device_id_type=MESH,
+    )
+    gm_copy.start()
     for layer in range(layers):
         for t in range(DP - 1):
             rs_copy(layer, t).wait_send()
             ag_copy(layer, t + 1).wait_send()
-    kvg_out = pltpu.make_async_copy(kvg, kvg_hbm, out_sem.at[3])
-    gm_out = pltpu.make_async_copy(gm_v, gm_hbm, out_sem.at[4])
-    kvg_out.start()
-    gm_out.start()
-    for copy in (mem_out, att_out, gq_out, kvg_out, gm_out):
+    gm_copy.wait()
+    gm_landed[...] += gm_v[core]
+    gm_outs = [
+        pltpu.make_async_copy(gm_landed.at[(z + k) % CHIPS], hbm, out_sem.at[4 + k])
+        for k, hbm in enumerate((gm0_hbm, gm1_hbm, gm2_hbm, gm3_hbm))
+    ]
+    for copy in gm_outs:
+        copy.start()
+    for copy in [mem_out, att_out, gq_out, kvg_out] + gm_outs:
         copy.wait()
 
 
@@ -283,25 +317,21 @@
         jax.ShapeDtypeStruct(queries.shape, BF16),
         jax.ShapeDtypeStruct((layers, 2, width, mem_total), BF16),
         jax.ShapeDtypeStruct((DP, CORES, CHIPS, tokens, quarter), BF16),
-        jax.ShapeDtypeStruct((mem_total, quarter), F32),
-    )
+    ) + (jax.ShapeDtypeStruct((tokens, quarter), F32),) * CHIPS
     return pl.pallas_call(
         attention_kernel,
         out_shape=out_shape,
-        in_specs=[
-            any_spec,
-            pl.BlockSpec(memory_space=pltpu.VMEM),
-            any_spec,
-            any_spec,
-            any_spec,
-        ],
-        out_specs=(any_spec,) * 5,
+        in_specs=[any_spec, pl.BlockSpec(memory_space=pltpu.HBM)] + [any_spec] * 3,
+        out_specs=(any_spec,) * (4 + CHIPS),
         scratch_shapes=[
             pltpu.VMEM(queries.shape, BF16),
             pltpu.VMEM(queries.shape, BF16),
+            pltpu.VMEM((layers, width, rows), BF16),
+            pltpu.VMEM((layers, width, rows), BF16),
             pltpu.VMEM(queries.shape, BF16),
             pltpu.VMEM(queries.shape, BF16),
             pltpu.VMEM((layers, 2, width, model), BF16),
+            pltpu.VMEM(memory.shape, BF16),
             pltpu.VMEM((DP, CORES, CHIPS, tokens, quarter), BF16),
             pltpu.VMEM((layers, 2, width, mem_total), F32),
             pltpu.VMEM((layers, 2, width, mem_total), BF16),
@@ -309,10 +339,11 @@
             pltpu.VMEM((layers, 2, PAIR, mem_total), F32),
             pltpu.VMEM((layers, DP - 1, 2, PAIR, mem_total), BF16),
             pltpu.VMEM((layers, 2, width, mem_total), BF16),
-            pltpu.VMEM((mem_total, quarter), F32),
-            dma((2,)),
+            pltpu.VMEM((CORES, CHIPS, tokens, quarter), F32),
+            pltpu.VMEM((CHIPS, tokens, quarter), F32),
+            dma((3,)),
             dma((DP, 2)),
-            dma((5,)),
+            dma((4 + CHIPS,)),
             dma((CHIPS - 1,)),
             dma((CHIPS - 1,)),
             dma((DP - 1,)),
@@ -323,6 +354,7 @@
             dma((layers, DP - 1)),
             dma((layers, DP - 1)),
             dma((layers, DP - 1)),
+            dma((2,)),
         ],
         compiler_params=pltpu.CompilerParams(
             collective_id=0, has_side_effects=True, vmem_limit_bytes=52 * 2**20
@@ -334,55 +366,74 @@
     )(queries, memory, w_key, w_value, grad_out)
 
 
-def weight_kernel(kvg_ref, mem_ref, gwk_ref, gwv_ref):
+def weight_kernel(kvg_ref, mem_ref, out_ref):
     quarter = mem_ref.shape[-1]
-    for kv, out in enumerate((gwk_ref, gwv_ref)):
-        for j in range(DP):
-            out[0, :, j * quarter : (j + 1) * quarter] = jnp.dot(
-                kvg_ref[0, kv], mem_ref[j], preferred_element_type=F32
-            )
-
-
-def weight_gradients(kvg, mem):
+    for j in range(DP):
+        out_ref[0, :, j * quarter : (j + 1) * quarter] = jnp.dot(
+            kvg_ref[0, 0], mem_ref[j], preferred_element_type=F32
+        )
+
+
+def weight_gradient(kvg, mem, kv):
     layers, _, width, mem_total = kvg.shape
     quarter = mem.shape[-1]
     model = DP * quarter
-    rows = 128
-    out = jax.ShapeDtypeStruct((layers, width, model), F32)
+    rows = 256
     return pl.pallas_call(
         weight_kernel,
         grid=(layers, width // rows),
         in_specs=[
-            pl.BlockSpec((1, 2, rows, mem_total), lambda l, c: (l, 0, c, 0)),
+            pl.BlockSpec((1, 1, rows, mem_total), lambda l, c: (l, kv, c, 0)),
             pl.BlockSpec((DP, mem_total, quarter), lambda l, c: (0, 0, 0)),
         ],
-        out_specs=[pl.BlockSpec((1, rows, model), lambda l, c: (l, c, 0))] * 2,
-        out_shape=(out, out),
+        out_specs=pl.BlockSpec((1, rows, model), lambda l, c: (l, c, 0)),
+        out_shape=jax.ShapeDtypeStruct((layers, width, model), F32),
         compiler_params=pltpu.CompilerParams(vmem_limit_bytes=32 * 2**20),
         cost_estimate=pl.CostEstimate(
-            flops=4 * layers * width * mem_total * model,
-            bytes_accessed=8 * layers * width * model,
+            flops=2 * layers * width * mem_total * model,
+            bytes_accessed=4 * layers * width * model,
             transcendentals=0,
         ),
-        name="weight_gradients",
+        name=("grad_w_key", "grad_w_value")[kv],
     )(kvg, mem)
 
 
+def place_kernel(*refs):
+    out_ref = refs[-1]
+    quarter = refs[0].shape[-1]
+    i = lax.axis_index("dp")
+    for k, ref in enumerate(refs[:-1]):
+        j = (i + DP - k) % DP
+        out_ref[:, pl.ds(pl.multiple_of(j * quarter, quarter), quarter)] = ref[...]
+
+
 def fused_shards(queries, memory, w_key, w_value, grad_out):
-    attended, grad_queries, kvg, mem, gm_part = attention(
+    attended, grad_queries, kvg, mem, *gm_parts = attention(
         queries, memory, w_key, w_value, grad_out
     )
-    tokens = memory.shape[0]
-    mem_total = tokens * CHIPS * CORES
-    quarter = mem.shape[-1]
-    gm_part = (
-        gm_part.reshape(CORES, CHIPS, tokens, quarter)
-        .transpose(1, 0, 2, 3)
-        .reshape(mem_total, quarter)
-    )
-    gm = lax.psum_scatter(gm_part, "mp", scatter_dimension=0, tiled=True)
-    grad_memory = lax.all_gather(gm, "dp", axis=1, tiled=True)
-    grad_w_key, grad_w_value = weight_gradients(kvg, mem.reshape(DP, mem_total, quarter))
+    tokens, model = memory.shape
+    mem = mem.reshape(DP, tokens * CHIPS * CORES, model // DP)
+    gm = gm_parts[0]
+    for k in range(1, CHIPS):
+        ring = [
+            (z * CORES + core, (z + k) % CHIPS * CORES + core)
+            for z in range(CHIPS)
+            for core in range(CORES)
+        ]
+        gm = gm + lax.ppermute(gm_parts[k], "mp", ring)
+    grad_w_key = weight_gradient(kvg, mem, 0)
+    grad_w_key, gm = lax.optimization_barrier((grad_w_key, gm))
+    quarters = [gm] + [
+        lax.ppermute(gm, "dp", [(i, (i + k) % DP) for i in range(DP)]) for k in range(1, DP)
+    ]
+    grad_w_value = weight_gradient(kvg, mem, 1)
+    grad_memory = pl.pallas_call(
+        place_kernel,
+        in_specs=[pl.BlockSpec(memory_space=pltpu.VMEM)] * DP,
+        out_specs=pl.BlockSpec(memory_space=pltpu.VMEM),
+        out_shape=jax.ShapeDtypeStruct((tokens, model), F32),
+        name="place",
+    )(*quarters)
     return attended, grad_queries, grad_memory, grad_w_key, grad_w_value
 
 

time: 110 us -> 87.6 us (0.80)
  waiting for transfers between devices: 13.9 us -> 0.02 us
  between operations: 14.1 us -> 0.71 us
  blocking collectives: 9.16 us -> 0 us
  starting transfers between devices: 0.04 us -> 7.6 us
  Pallas kernels: 66 us -> 72.5 us
    reduce_scatter x1 -> x0, waiting for transfers between devices: 13.9 us -> none  [fused_shards(): gm = lax.psum_scatter(gm_part, 'mp', scatter_dimension=0, tiled=True)]
    all_gather x1 -> x0, blocking collectives: 9.16 us -> none  [fused_shards(): grad_memory = lax.all_gather(gm, 'dp', axis=1, tiled=True)]
    ppermute x0 -> x6, starting transfers between devices: none -> 7.6 us  [the longest x3 4.77 us: fused_shards(): gm = gm + lax.ppermute(gm_parts[k], 'mp', ring)]
    pallas_call x1 -> x3, Pallas kernels: 16.5 us -> 20.7 us  [the longest x2 19 us: weight_gradient(): pl.pallas_call(weight_kernel, grid=(layers, width // rows), in_specs=[pl....]
    pallas_call x1, Pallas kernels: 49.5 us -> 51.9 us  [attention(): pl.pallas_call(attention_kernel, out_shape=out_shape, in_specs=[any_spec,...]
    unnamed x11 -> x18, local copies, waits for them, and re-layouts: 5.25 us -> 6.5 us
  transfers between devices with their start and end apart: 1 -> 6, of which waited for: 1 -> 0; matrix products, arithmetic and copies ran while one was open for 0% -> 0% of each run, Pallas kernels for 15% -> 22%
where the time goes in v2:
time: 87.6 us; the launch traced here: 87.4 us
  Pallas kernels  72.5 us (83%)
  starting transfers between devices  7.6 us (9%)
  local copies, waits for them, and re-layouts  6.5 us (7%)
    pallas_call x1, Pallas kernels, attention(): pl.pallas_call(attention_kernel, out_shape=out_shape, in_specs=[any_spec,...  51.9 us
    pallas_call x2, Pallas kernels, weight_gradient(): pl.pallas_call(weight_kernel, grid=(layers, width // rows), in_specs=[pl....  19 us
    unnamed x18, local copies, waits for them, and re-layouts  6.5 us
    ppermute x3, starting transfers between devices, fused_shards(): gm = gm + lax.ppermute(gm_parts[k], 'mp', ring)  4.77 us
    ppermute x3, starting transfers between devices, fused_shards(): lax.ppermute(gm, 'dp', [(i, (i + k) % DP) for i in range(DP)])  2.83 us
  transfers between devices with their start and end apart: 6, of which 0 were waited for; matrix products, arithmetic and copies ran while one was open for 0% of the time, Pallas kernels for 22%

profile of v2, /device:TPU:0, one launch (start us, length us, event | category | flops | bytes accessed | tf_op | source)
XLA Modules:
  0.0 87.4 jit_solution(8591704006647650662)
XLA Ops:
  0.6 0.0 copy-start.1
  0.6 0.9 %copy-done.1 = bf16[16,4096]{1,0:T(8,128)(2,1)S(1)} copy-done((bf16[16,4096]{1,0:T(8,128)(2,1)S(1)}, bf16[16,4096]{1,0:T(8,128)(2,1)}, u32[]{:S(2)}) %copy-start.1) | copy-done | bytes 131096
  1.5 51.9 %attention.1 = (bf16[3,512,512]{2,1,0:T(8,128)(2,1)}, bf16[3,512,512]{2,1,0:T(8,128)(2,1)}, bf16[3,2,512,128]{3,2,1,0:T(8,128)(2,1)S(1)}, bf16[4,2,4,16,1024]{4,...) custom-call(bf16[3,512,512]{2,1,0:T(8,128)(2,1)} %q_hbm.1, ...), custom_call_target="tpu_custom_call" | custom-call | flops 8000000000 | bytes 35000000 | tf_op jit(solution)/shard_map/attention/pallas_call | solution.py:321
  53.4 1.4 %collective-permute-start = (f32[16,1024]{1,0:T(8,128)S(1)}, f32[16,1024]{1,0:T(8,128)S(1)}, u32[]{:S(2)}, u32[]{:S(2)}) collective-permute-start(f32[16,1024]{1,0:T(8,128)S(1)} %get-tuple-element.20), channel_id=1, source_target_pairs={{0,2},{1,3},{2,4},{3,5},{4,6},{5,7},{6,0},{7,1},{8,10},{9,11},{10,... | collective-permute-start | bytes 196616 | tf_op jit(solution)/shard_map/ppermute | solution.py:423
  54.8 2.3 %collective-permute-start.1 = (f32[16,1024]{1,0:T(8,128)S(1)}, f32[16,1024]{1,0:T(8,128)S(1)}, u32[]{:S(2)}, u32[]{:S(2)}) collective-permute-start(f32[16,1024]{1,0:T(8,128)S(1)} %get-tuple-element.21), channel_id=1, source_target_pairs={{0,4},{1,5},{2,6},{3,7},{4,0},{5,1},{6,2},{7,3},{8,12},{9,13},{10,... | collective-permute-start | bytes 196616 | tf_op jit(solution)/shard_map/ppermute | solution.py:423
  57.1 1.1 %collective-permute-start.2 = (f32[16,1024]{1,0:T(8,128)S(1)}, f32[16,1024]{1,0:T(8,128)S(1)}, u32[]{:S(2)}, u32[]{:S(2)}) collective-permute-start(f32[16,1024]{1,0:T(8,128)S(1)} %get-tuple-element.22), channel_id=1, source_target_pairs={{0,6},{1,7},{2,0},{3,1},{4,2},{5,3},{6,4},{7,5},{8,14},{9,15},{10,... | collective-permute-start | bytes 196616 | tf_op jit(solution)/shard_map/ppermute | solution.py:423
  58.2 0.0 copy-start
  58.2 1.2 %copy-done = bf16[4,2,4,16,1024]{4,3,2,1,0:T(8,128)(2,1)S(1)} copy-done((bf16[4,2,4,16,1024]{4,3,2,1,0:T(8,128)(2,1)S(1)}, bf16[4,2,4,16,1024]{4,3,2,1,0:T(8,128)(2,1)}, u32[]{:S(2)}) %copy-start) | copy-done | bytes 1048600
  59.4 9.5 %grad_w_key.1 = f32[3,512,4096]{2,1,0:T(8,128)} custom-call(bf16[3,2,512,128]{3,2,1,0:T(8,128)(2,1)S(1)} %get-tuple-element.17.kvg_ref, bf16[4,128,1024]{2,1,0:T(8,128)(2,1)S(1)} %bitcast.1), custom_call_target="tpu_custom_call" | custom-call | flops 1610612736 | bytes 25165824 | tf_op jit(solution)/shard_map/grad_w_key/pallas_call | solution.py:382
  68.9 0.0 collective-permute-done
  68.9 0.0 collective-permute-done.1
  68.9 0.0 collective-permute-done.2
  68.9 0.0 copy-start.4
  68.9 1.5 %collective-permute-start.5 = (f32[16,1024]{1,0:T(8,128)S(1)}, f32[16,1024]{1,0:T(8,128)S(1)}, u32[]{:S(2)}, u32[]{:S(2)}) collective-permute-start(f32[16,1024]{1,0:T(8,128)S(1)} %add_add_fusion.refs_0_), channel_id=1, source_target_pairs={{0,24},{8,0},{16,8},{24,16},{1,25},{9,1},{17,9},{25,17},{2,26},{10... | collective-permute-start | bytes 196616 | tf_op jit(solution)/shard_map/ppermute | solution.py:427
  70.5 0.7 collective-permute-start.4
  71.1 0.7 collective-permute-start.3
  71.8 0.0 copy-start.3
  71.8 9.5 %grad_w_value.1 = f32[3,512,4096]{2,1,0:T(8,128)} custom-call(bf16[3,2,512,128]{3,2,1,0:T(8,128)(2,1)S(1)} %get-tuple-element.17.kvg_ref, bf16[4,128,1024]{2,1,0:T(8,128)(2,1)S(1)} %bitcast.2), custom_call_target="tpu_custom_call" | custom-call | flops 1610612736 | bytes 25165824 | tf_op jit(solution)/shard_map/grad_w_value/pallas_call | solution.py:382
  81.3 0.0 copy-done.4
  81.3 0.0 collective-permute-done.5.refs_3_
  81.3 0.0 copy-start.5
  81.3 0.0 collective-permute-done.4.refs_2_
  81.3 0.0 copy-start.6
  81.3 0.0 collective-permute-done.3.refs_1_
  81.3 0.6 copy-done.5
  81.9 0.0 copy-done.6
  81.9 0.6 copy-done.7
  82.6 1.7 %place.1 = f32[16,4096]{1,0:T(8,128)} custom-call(f32[16,1024]{1,0:T(8,128)} %copy-done.4, f32[16,1024]{1,0:T(8,128)} %copy-done.7, f32[16,1024]{1,0:T(8,128)} %copy-done.6, f32[16,1024]{1,0:T(8,128)} %copy-done.5), custom_call_target="tpu_custom_call" | custom-call | tf_op jit(solution)/shard_map/place/pallas_call | solution.py:430
  84.2 0.0 copy-done.3
  84.2 1.1 %copy.12 = bf16[3,512,512]{2,1,0:T(8,128)(2,1)} copy(bf16[3,512,512]{2,1,0:T(8,128)(2,1)S(1)} %copy-done.3) | data formatting | bytes 3145728
  85.4 0.8 copy-done.2
  86.2 1.1 %copy.13 = bf16[3,512,512]{2,1,0:T(8,128)(2,1)} copy(bf16[3,512,512]{2,1,0:T(8,128)(2,1)S(1)} %copy-done.2) | data formatting | bytes 3145728
  (3 shorter events, 0.0 us)
Async XLA Ops:
  0.6 0.9 %copy-start.1 = (bf16[16,4096]{1,0:T(8,128)(2,1)S(1)}, bf16[16,4096]{1,0:T(8,128)(2,1)}, u32[]{:S(2)}) copy-start(bf16[16,4096]{1,0:T(8,128)(2,1)} %mem_in.1) | copy-start | bytes 393220
  53.4 15.5 %collective-permute-start = (f32[16,1024]{1,0:T(8,128)S(1)}, f32[16,1024]{1,0:T(8,128)S(1)}, u32[]{:S(2)}, u32[]{:S(2)}) collective-permute-start(f32[16,1024]{1,0:T(8,128)S(1)} %get-tuple-element.20), channel_id=1, source_target_pairs={{0,2},{1,3},{2,4},{3,5},{4,6},{5,7},{6,0},{7,1},{8,10},{9,11},{10,... | collective-permute-start | bytes 196616 | tf_op jit(solution)/shard_map/ppermute | solution.py:423
  54.8 14.1 %collective-permute-start.1 = (f32[16,1024]{1,0:T(8,128)S(1)}, f32[16,1024]{1,0:T(8,128)S(1)}, u32[]{:S(2)}, u32[]{:S(2)}) collective-permute-start(f32[16,1024]{1,0:T(8,128)S(1)} %get-tuple-element.21), channel_id=1, source_target_pairs={{0,4},{1,5},{2,6},{3,7},{4,0},{5,1},{6,2},{7,3},{8,12},{9,13},{10,... | collective-permute-start | bytes 196616 | tf_op jit(solution)/shard_map/ppermute | solution.py:423
  57.1 11.8 %collective-permute-start.2 = (f32[16,1024]{1,0:T(8,128)S(1)}, f32[16,1024]{1,0:T(8,128)S(1)}, u32[]{:S(2)}, u32[]{:S(2)}) collective-permute-start(f32[16,1024]{1,0:T(8,128)S(1)} %get-tuple-element.22), channel_id=1, source_target_pairs={{0,6},{1,7},{2,0},{3,1},{4,2},{5,3},{6,4},{7,5},{8,14},{9,15},{10,... | collective-permute-start | bytes 196616 | tf_op jit(solution)/shard_map/ppermute | solution.py:423
  58.2 1.2 %copy-start = (bf16[4,2,4,16,1024]{4,3,2,1,0:T(8,128)(2,1)S(1)}, bf16[4,2,4,16,1024]{4,3,2,1,0:T(8,128)(2,1)}, u32[]{:S(2)}) copy-start(bf16[4,2,4,16,1024]{4,3,2,1,0:T(8,128)(2,1)} %get-tuple-element.18) | copy-start | bytes 3145732
  68.9 12.3 %copy-start.4 = (f32[16,1024]{1,0:T(8,128)}, f32[16,1024]{1,0:T(8,128)S(1)}, u32[]{:S(2)}) copy-start(f32[16,1024]{1,0:T(8,128)S(1)} %add_add_fusion.refs_0_) | copy-start | bytes 196612
  68.9 12.3 %collective-permute-start.5 = (f32[16,1024]{1,0:T(8,128)S(1)}, f32[16,1024]{1,0:T(8,128)S(1)}, u32[]{:S(2)}, u32[]{:S(2)}) collective-permute-start(f32[16,1024]{1,0:T(8,128)S(1)} %add_add_fusion.refs_0_), channel_id=1, source_target_pairs={{0,24},{8,0},{16,8},{24,16},{1,25},{9,1},{17,9},{25,17},{2,26},{10... | collective-permute-start | bytes 196616 | tf_op jit(solution)/shard_map/ppermute | solution.py:427
  70.5 10.8 %collective-permute-start.4 = (f32[16,1024]{1,0:T(8,128)S(1)}, f32[16,1024]{1,0:T(8,128)S(1)}, u32[]{:S(2)}, u32[]{:S(2)}) collective-permute-start(f32[16,1024]{1,0:T(8,128)S(1)} %add_add_fusion.refs_0_), channel_id=1, source_target_pairs={{0,16},{8,24},{16,0},{24,8},{1,17},{9,25},{17,1},{25,9},{2,18},{10... | collective-permute-start | bytes 196616 | tf_op jit(solution)/shard_map/ppermute | solution.py:427
  71.1 10.2 %collective-permute-start.3 = (f32[16,1024]{1,0:T(8,128)S(1)}, f32[16,1024]{1,0:T(8,128)S(1)}, u32[]{:S(2)}, u32[]{:S(2)}) collective-permute-start(f32[16,1024]{1,0:T(8,128)S(1)} %add_add_fusion.refs_0_), channel_id=1, source_target_pairs={{0,8},{8,16},{16,24},{24,0},{1,9},{9,17},{17,25},{25,1},{2,10},{10... | collective-permute-start | bytes 196616 | tf_op jit(solution)/shard_map/ppermute | solution.py:427
  71.8 12.5 %copy-start.3 = (bf16[3,512,512]{2,1,0:T(8,128)(2,1)S(1)}, bf16[3,512,512]{2,1,0:T(8,128)(2,1)}, u32[]{:S(2)}) copy-start(bf16[3,512,512]{2,1,0:T(8,128)(2,1)} %get-tuple-element.30) | copy-start | bytes 4718596
  81.3 0.6 copy-start.5
  81.3 0.6 copy-start.6
  81.9 0.6 copy-start.7
  84.2 2.0 %copy-start.2 = (bf16[3,512,512]{2,1,0:T(8,128)(2,1)S(1)}, bf16[3,512,512]{2,1,0:T(8,128)(2,1)}, u32[]{:S(2)}) copy-start(bf16[3,512,512]{2,1,0:T(8,128)(2,1)} %get-tuple-element.31) | copy-start | bytes 4718596

commit v3 on v2

--- a/solution.py
+++ b/solution.py
@@ -17,7 +17,7 @@
 def attention_kernel(
     q_hbm, mem_in, wk_hbm, wv_hbm, g_hbm,
     att_hbm, gq_hbm, kvg_hbm, mem_hbm, gm0_hbm, gm1_hbm, gm2_hbm, gm3_hbm,
-    q_v, g_v, qt_v, gt_v, att_v, gq_v, w_v, mem_ref, mg, acc, kvt, part, own, landed, kvg,
+    q_v, g_v, qt_v, gt_v, att_t, gq_t, w_v, mem_ref, mg, acc, kvt, part, own, landed, kvg,
     gm_v, gm_landed,
     in_sem, w_sem, out_sem, z_send, z_recv, d_send, d_recv, s_send, s_recv,
     rs_send, rs_recv, ag_send, ag_recv, gm_sem,
@@ -184,52 +184,59 @@
         for k in range(1, DP):
             ag_copy(layer, k).start()
 
-    first_head = lax.broadcasted_iota(jnp.int32, (PAIR, mem_total), 0) < HEAD_WIDTH
-
-    def block_diagonal(block):
+    def head_masks(axis):
+        return lax.broadcasted_iota(jnp.int32, (PAIR, PAIR), axis) < HEAD_WIDTH
+
+    first_row, first_lane = head_masks(0), head_masks(1)
+
+    def split_heads(block, mask, axis):
         zero = jnp.zeros_like(block)
         return jnp.concatenate(
-            [jnp.where(first_head, block, zero), jnp.where(first_head, zero, block)], axis=1
+            [jnp.where(mask, block, zero), jnp.where(mask, zero, block)], axis=axis
         )
 
     def own_blocks(both):
-        return jnp.where(first_head, both[:, :mem_total], both[:, mem_total:])
+        return jnp.where(first_row, both[:, :mem_total], both[:, mem_total:])
+
+    def dot_nt(lhs, rhs):
+        return lax.dot_general(lhs, rhs, (((1,), (1,)), ((), ())), preferred_element_type=F32)
 
     def attend(layer, t):
-        pair = (i + 1 + t) % DP
-        lanes = pair_rows(pair)
-        queries = q_v[layer, :, lanes]
-        grads = g_v[layer, :, lanes]
-        keys = block_diagonal(kvt[layer, 0, lanes, :])
-        values = block_diagonal(kvt[layer, 1, lanes, :])
-        scores = jnp.dot(queries, keys, preferred_element_type=F32)
-        grad_probs = jnp.dot(grads, values, preferred_element_type=F32)
+        lanes = pair_rows((i + 1 + t) % DP)
+        queries, grads = qt_v[layer, lanes, :], gt_v[layer, lanes, :]
+        keys, values = kvt[layer, 0, lanes, :], kvt[layer, 1, lanes, :]
+        scores = jnp.dot(
+            split_heads(keys.T, first_lane, 0), queries, preferred_element_type=F32
+        )
+        grad_probs = jnp.dot(
+            split_heads(values.T, first_lane, 0), grads, preferred_element_type=F32
+        )
         probs_b, grad_scores = [], []
         for head in range(2):
-            at = slice(head * mem_total, (head + 1) * mem_total)
-            s = scores[:, at]
-            gp = grad_probs[:, at]
-            e = jnp.exp(s - jnp.max(s, axis=-1, keepdims=True))
-            probs = e * (1.0 / jnp.sum(e, axis=-1, keepdims=True))
-            delta = jnp.sum(probs * gp, axis=-1, keepdims=True)
-            probs_b.append(probs.astype(BF16))
-            grad_scores.append((probs * (gp - delta)).astype(BF16))
-        probs_b = jnp.concatenate(probs_b, axis=1)
-        grad_scores = jnp.concatenate(grad_scores, axis=1)
-        nt = (((1,), (1,)), ((), ()))
-        att_v[layer, :, lanes] = lax.dot_general(
-            probs_b, values, nt, preferred_element_type=F32
+            probs_row, grads_row = [], []
+            for chunk in range(rows // 128):
+                at = (
+                    slice(head * mem_total, (head + 1) * mem_total),
+                    slice(chunk * 128, (chunk + 1) * 128),
+                )
+                s, gp = scores[at], grad_probs[at]
+                e = jnp.exp(s - jnp.max(s, axis=0, keepdims=True))
+                scale = 1.0 / jnp.sum(e, axis=0, keepdims=True)
+                delta = jnp.sum(e * gp, axis=0, keepdims=True) * scale
+                probs = e * scale
+                probs_row.append(probs.astype(BF16))
+                grads_row.append((probs * (gp - delta)).astype(BF16))
+            probs_b.append(jnp.concatenate(probs_row, axis=1))
+            grad_scores.append(jnp.concatenate(grads_row, axis=1))
+        probs_b = jnp.concatenate(probs_b, axis=0)
+        grad_scores = jnp.concatenate(grad_scores, axis=0)
+        att_t[layer, lanes, :] = jnp.dot(
+            split_heads(values, first_row, 1), probs_b, preferred_element_type=F32
         ).astype(BF16)
-        gq_v[layer, :, lanes] = lax.dot_general(
-            grad_scores, keys, nt, preferred_element_type=F32
+        gq_t[layer, lanes, :] = jnp.dot(
+            split_heads(keys, first_row, 1), grad_scores, preferred_element_type=F32
         ).astype(BF16)
-        grad_keys = own_blocks(
-            jnp.dot(qt_v[layer, lanes, :], grad_scores, preferred_element_type=F32)
-        )
-        grad_values = own_blocks(
-            jnp.dot(gt_v[layer, lanes, :], probs_b, preferred_element_type=F32)
-        )
-        return grad_keys, grad_values
+        return own_blocks(dot_nt(queries, grad_scores)), own_blocks(dot_nt(grads, probs_b))
 
     def send_part(layer, t, grads):
         for kv in range(2):
@@ -250,11 +257,6 @@
         send_part(layer, 2, third)
         for kv in range(2):
             own[layer, kv] = last[kv]
-
-    att_out = pltpu.make_async_copy(att_v, att_hbm, out_sem.at[1])
-    gq_out = pltpu.make_async_copy(gq_v, gq_hbm, out_sem.at[2])
-    att_out.start()
-    gq_out.start()
 
     def add_memory_gradient(layer):
         for k in range(1, DP):
@@ -271,13 +273,22 @@
             else:
                 gm_v[...] += term
 
-    for layer in range(layers):
-        if layer == layers - 1:
-            reduce(layer)
-            add_memory_gradient(layer - 1)
-            add_memory_gradient(layer)
-        elif layer < layers - 2:
-            add_memory_gradient(layer)
+    for layer in range(layers - 2):
+        add_memory_gradient(layer)
+    reduce(layers - 1)
+
+    @pl.loop(0, layers * DP)
+    def turn_back(n):
+        lanes = pair_rows(n % DP)
+        q_v[n // DP, :, lanes] = att_t[n // DP, lanes, :].T
+        g_v[n // DP, :, lanes] = gq_t[n // DP, lanes, :].T
+
+    att_out = pltpu.make_async_copy(q_v, att_hbm, out_sem.at[1])
+    gq_out = pltpu.make_async_copy(g_v, gq_hbm, out_sem.at[2])
+    att_out.start()
+    gq_out.start()
+    for layer in range(max(layers - 2, 0), layers):
+        add_memory_gradient(layer)
     kvg_out = pltpu.make_async_copy(kvg, kvg_hbm, out_sem.at[3])
     kvg_out.start()
     gm_copy = pltpu.make_async_remote_copy(
@@ -328,8 +339,8 @@
             pltpu.VMEM(queries.shape, BF16),
             pltpu.VMEM((layers, width, rows), BF16),
             pltpu.VMEM((layers, width, rows), BF16),
-            pltpu.VMEM(queries.shape, BF16),
-            pltpu.VMEM(queries.shape, BF16),
+            pltpu.VMEM((layers, width, rows), BF16),
+            pltpu.VMEM((layers, width, rows), BF16),
             pltpu.VMEM((layers, 2, width, model), BF16),
             pltpu.VMEM(memory.shape, BF16),
             pltpu.VMEM((DP, CORES, CHIPS, tokens, quarter), BF16),
@@ -378,7 +389,7 @@
     layers, _, width, mem_total = kvg.shape
     quarter = mem.shape[-1]
     model = DP * quarter
-    rows = 256
+    rows = 128
     return pl.pallas_call(
         weight_kernel,
         grid=(layers, width // rows),
@@ -515,7 +526,8 @@
             mesh.shape["dp"] == DP
             and mesh.shape["mp"] == CHIPS * CORES
             and queries.shape[2] == DP * PAIR
-            and memory.shape[0] == 16
+            and queries.shape[1] % (128 * DP) == 0
+            and memory.shape[0] == PAIR // (CHIPS * CORES)
             and memory.shape[1] % (DP * 128) == 0
         )
         run = fused_shards if fits else shards

time: 87.6 us -> 90.6 us (1.034)
  Pallas kernels: 72.5 us -> 75.5 us
    pallas_call x2, Pallas kernels: 19 us -> 22.2 us  [weight_gradient(): pl.pallas_call(weight_kernel, grid=(layers, width // rows), in_specs=[pl....]
  transfers between devices with their start and end apart: 6 -> 6, of which waited for: 0 -> 0; matrix products, arithmetic and copies ran while one was open for 0% -> 0% of each run, Pallas kernels for 22% -> 25%
where the time goes in v3:
time: 90.6 us; the launch traced here: 90.3 us
  Pallas kernels  75.5 us (83%)
  starting transfers between devices  7.6 us (8%)
  local copies, waits for them, and re-layouts  6.5 us (7%)
    pallas_call x1, Pallas kernels, attention(): pl.pallas_call(attention_kernel, out_shape=out_shape, in_specs=[any_spec,...  51.6 us
    pallas_call x2, Pallas kernels, weight_gradient(): pl.pallas_call(weight_kernel, grid=(layers, width // rows), in_specs=[pl....  22.2 us
    unnamed x18, local copies, waits for them, and re-layouts  6.5 us
    ppermute x3, starting transfers between devices, fused_shards(): gm = gm + lax.ppermute(gm_parts[k], 'mp', ring)  4.77 us
    ppermute x3, starting transfers between devices, fused_shards(): lax.ppermute(gm, 'dp', [(i, (i + k) % DP) for i in range(DP)])  2.84 us
  transfers between devices with their start and end apart: 6, of which 0 were waited for; matrix products, arithmetic and copies ran while one was open for 0% of the time, Pallas kernels for 25%

profile of v3, /device:TPU:0, one launch (start us, length us, event | category | flops | bytes accessed | tf_op | source)
XLA Modules:
  0.0 90.3 jit_solution(14638581678657723291)
XLA Ops:
  0.6 0.0 copy-start.1
  0.6 0.9 copy-done.1
  1.5 51.6 %attention.1 = (bf16[3,512,512]{2,1,0:T(8,128)(2,1)}, bf16[3,512,512]{2,1,0:T(8,128)(2,1)}, bf16[3,2,512,128]{3,2,1,0:T(8,128)(2,1)S(1)}, bf16[4,2,4,16,1024]{4,...) custom-call(bf16[3,512,512]{2,1,0:T(8,128)(2,1)} %q_hbm.1, ...), custom_call_target="tpu_custom_call" | custom-call | flops 8000000000 | bytes 35000000 | tf_op jit(solution)/shard_map/attention/pallas_call | solution.py:332
  53.1 1.4 %collective-permute-start = (f32[16,1024]{1,0:T(8,128)S(1)}, f32[16,1024]{1,0:T(8,128)S(1)}, u32[]{:S(2)}, u32[]{:S(2)}) collective-permute-start(f32[16,1024]{1,0:T(8,128)S(1)} %get-tuple-element.20), channel_id=1, source_target_pairs={{0,2},{1,3},{2,4},{3,5},{4,6},{5,7},{6,0},{7,1},{8,10},{9,11},{10,... | collective-permute-start | bytes 196616 | tf_op jit(solution)/shard_map/ppermute | solution.py:434
  54.5 2.3 %collective-permute-start.1 = (f32[16,1024]{1,0:T(8,128)S(1)}, f32[16,1024]{1,0:T(8,128)S(1)}, u32[]{:S(2)}, u32[]{:S(2)}) collective-permute-start(f32[16,1024]{1,0:T(8,128)S(1)} %get-tuple-element.21), channel_id=1, source_target_pairs={{0,4},{1,5},{2,6},{3,7},{4,0},{5,1},{6,2},{7,3},{8,12},{9,13},{10,... | collective-permute-start | bytes 196616 | tf_op jit(solution)/shard_map/ppermute | solution.py:434
  56.8 1.1 %collective-permute-start.2 = (f32[16,1024]{1,0:T(8,128)S(1)}, f32[16,1024]{1,0:T(8,128)S(1)}, u32[]{:S(2)}, u32[]{:S(2)}) collective-permute-start(f32[16,1024]{1,0:T(8,128)S(1)} %get-tuple-element.22), channel_id=1, source_target_pairs={{0,6},{1,7},{2,0},{3,1},{4,2},{5,3},{6,4},{7,5},{8,14},{9,15},{10,... | collective-permute-start | bytes 196616 | tf_op jit(solution)/shard_map/ppermute | solution.py:434
  57.9 0.0 copy-start
  57.9 1.2 %copy-done = bf16[4,2,4,16,1024]{4,3,2,1,0:T(8,128)(2,1)S(1)} copy-done((bf16[4,2,4,16,1024]{4,3,2,1,0:T(8,128)(2,1)S(1)}, bf16[4,2,4,16,1024]{4,3,2,1,0:T(8,128)(2,1)}, u32[]{:S(2)}) %copy-start) | copy-done | bytes 1048600
  59.1 11.1 %grad_w_key.1 = f32[3,512,4096]{2,1,0:T(8,128)} custom-call(bf16[3,2,512,128]{3,2,1,0:T(8,128)(2,1)S(1)} %get-tuple-element.17.kvg_ref, bf16[4,128,1024]{2,1,0:T(8,128)(2,1)S(1)} %bitcast.1), custom_call_target="tpu_custom_call" | custom-call | flops 1610612736 | bytes 25165824 | tf_op jit(solution)/shard_map/grad_w_key/pallas_call | solution.py:393
  70.2 0.0 collective-permute-done
  70.2 0.0 collective-permute-done.1
  70.2 0.0 collective-permute-done.2
  70.3 0.0 copy-start.4
  70.3 1.5 %collective-permute-start.5 = (f32[16,1024]{1,0:T(8,128)S(1)}, f32[16,1024]{1,0:T(8,128)S(1)}, u32[]{:S(2)}, u32[]{:S(2)}) collective-permute-start(f32[16,1024]{1,0:T(8,128)S(1)} %add_add_fusion.refs_0_), channel_id=1, source_target_pairs={{0,24},{8,0},{16,8},{24,16},{1,25},{9,1},{17,9},{25,17},{2,26},{10... | collective-permute-start | bytes 196616 | tf_op jit(solution)/shard_map/ppermute | solution.py:438
  71.8 0.7 collective-permute-start.4
  72.5 0.6 collective-permute-start.3
  73.1 0.0 copy-start.3
  73.1 11.1 %grad_w_value.1 = f32[3,512,4096]{2,1,0:T(8,128)} custom-call(bf16[3,2,512,128]{3,2,1,0:T(8,128)(2,1)S(1)} %get-tuple-element.17.kvg_ref, bf16[4,128,1024]{2,1,0:T(8,128)(2,1)S(1)} %bitcast.2), custom_call_target="tpu_custom_call" | custom-call | flops 1610612736 | bytes 25165824 | tf_op jit(solution)/shard_map/grad_w_value/pallas_call | solution.py:393
  84.2 0.0 copy-done.4
  84.2 0.0 collective-permute-done.5.refs_3_
  84.2 0.0 copy-start.5
  84.3 0.0 collective-permute-done.4.refs_2_
  84.3 0.0 copy-start.6
  84.3 0.0 collective-permute-done.3.refs_1_
  84.3 0.6 copy-done.5
  84.9 0.0 copy-done.6
  84.9 0.6 copy-done.7
  85.5 1.7 %place.1 = f32[16,4096]{1,0:T(8,128)} custom-call(f32[16,1024]{1,0:T(8,128)} %copy-done.4, f32[16,1024]{1,0:T(8,128)} %copy-done.7, f32[16,1024]{1,0:T(8,128)} %copy-done.6, f32[16,1024]{1,0:T(8,128)} %copy-done.5), custom_call_target="tpu_custom_call" | custom-call | tf_op jit(solution)/shard_map/place/pallas_call | solution.py:441
  87.2 0.0 copy-done.3
  87.2 1.1 %copy.12 = bf16[3,512,512]{2,1,0:T(8,128)(2,1)} copy(bf16[3,512,512]{2,1,0:T(8,128)(2,1)S(1)} %copy-done.3) | data formatting | bytes 3145728
  88.3 0.8 copy-done.2
  89.2 1.1 %copy.13 = bf16[3,512,512]{2,1,0:T(8,128)(2,1)} copy(bf16[3,512,512]{2,1,0:T(8,128)(2,1)S(1)} %copy-done.2) | data formatting | bytes 3145728
  (3 shorter events, 0.0 us)
Async XLA Ops:
  0.6 0.9 %copy-start.1 = (bf16[16,4096]{1,0:T(8,128)(2,1)S(1)}, bf16[16,4096]{1,0:T(8,128)(2,1)}, u32[]{:S(2)}) copy-start(bf16[16,4096]{1,0:T(8,128)(2,1)} %mem_in.1) | copy-start | bytes 393220
  53.1 17.1 %collective-permute-start = (f32[16,1024]{1,0:T(8,128)S(1)}, f32[16,1024]{1,0:T(8,128)S(1)}, u32[]{:S(2)}, u32[]{:S(2)}) collective-permute-start(f32[16,1024]{1,0:T(8,128)S(1)} %get-tuple-element.20), channel_id=1, source_target_pairs={{0,2},{1,3},{2,4},{3,5},{4,6},{5,7},{6,0},{7,1},{8,10},{9,11},{10,... | collective-permute-start | bytes 196616 | tf_op jit(solution)/shard_map/ppermute | solution.py:434
  54.5 15.7 %collective-permute-start.1 = (f32[16,1024]{1,0:T(8,128)S(1)}, f32[16,1024]{1,0:T(8,128)S(1)}, u32[]{:S(2)}, u32[]{:S(2)}) collective-permute-start(f32[16,1024]{1,0:T(8,128)S(1)} %get-tuple-element.21), channel_id=1, source_target_pairs={{0,4},{1,5},{2,6},{3,7},{4,0},{5,1},{6,2},{7,3},{8,12},{9,13},{10,... | collective-permute-start | bytes 196616 | tf_op jit(solution)/shard_map/ppermute | solution.py:434
  56.8 13.5 %collective-permute-start.2 = (f32[16,1024]{1,0:T(8,128)S(1)}, f32[16,1024]{1,0:T(8,128)S(1)}, u32[]{:S(2)}, u32[]{:S(2)}) collective-permute-start(f32[16,1024]{1,0:T(8,128)S(1)} %get-tuple-element.22), channel_id=1, source_target_pairs={{0,6},{1,7},{2,0},{3,1},{4,2},{5,3},{6,4},{7,5},{8,14},{9,15},{10,... | collective-permute-start | bytes 196616 | tf_op jit(solution)/shard_map/ppermute | solution.py:434
  57.9 1.2 %copy-start = (bf16[4,2,4,16,1024]{4,3,2,1,0:T(8,128)(2,1)S(1)}, bf16[4,2,4,16,1024]{4,3,2,1,0:T(8,128)(2,1)}, u32[]{:S(2)}) copy-start(bf16[4,2,4,16,1024]{4,3,2,1,0:T(8,128)(2,1)} %get-tuple-element.18) | copy-start | bytes 3145732
  70.3 14.0 %copy-start.4 = (f32[16,1024]{1,0:T(8,128)}, f32[16,1024]{1,0:T(8,128)S(1)}, u32[]{:S(2)}) copy-start(f32[16,1024]{1,0:T(8,128)S(1)} %add_add_fusion.refs_0_) | copy-start | bytes 196612
  70.3 14.0 %collective-permute-start.5 = (f32[16,1024]{1,0:T(8,128)S(1)}, f32[16,1024]{1,0:T(8,128)S(1)}, u32[]{:S(2)}, u32[]{:S(2)}) collective-permute-start(f32[16,1024]{1,0:T(8,128)S(1)} %add_add_fusion.refs_0_), channel_id=1, source_target_pairs={{0,24},{8,0},{16,8},{24,16},{1,25},{9,1},{17,9},{25,17},{2,26},{10... | collective-permute-start | bytes 196616 | tf_op jit(solution)/shard_map/ppermute | solution.py:438
  71.8 12.5 %collective-permute-start.4 = (f32[16,1024]{1,0:T(8,128)S(1)}, f32[16,1024]{1,0:T(8,128)S(1)}, u32[]{:S(2)}, u32[]{:S(2)}) collective-permute-start(f32[16,1024]{1,0:T(8,128)S(1)} %add_add_fusion.refs_0_), channel_id=1, source_target_pairs={{0,16},{8,24},{16,0},{24,8},{1,17},{9,25},{17,1},{25,9},{2,18},{10... | collective-permute-start | bytes 196616 | tf_op jit(solution)/shard_map/ppermute | solution.py:438
  72.5 11.8 %collective-permute-start.3 = (f32[16,1024]{1,0:T(8,128)S(1)}, f32[16,1024]{1,0:T(8,128)S(1)}, u32[]{:S(2)}, u32[]{:S(2)}) collective-permute-start(f32[16,1024]{1,0:T(8,128)S(1)} %add_add_fusion.refs_0_), channel_id=1, source_target_pairs={{0,8},{8,16},{16,24},{24,0},{1,9},{9,17},{17,25},{25,1},{2,10},{10... | collective-permute-start | bytes 196616 | tf_op jit(solution)/shard_map/ppermute | solution.py:438
  73.1 14.1 %copy-start.3 = (bf16[3,512,512]{2,1,0:T(8,128)(2,1)S(1)}, bf16[3,512,512]{2,1,0:T(8,128)(2,1)}, u32[]{:S(2)}) copy-start(bf16[3,512,512]{2,1,0:T(8,128)(2,1)} %get-tuple-element.30) | copy-start | bytes 4718596
  84.2 0.6 copy-start.5
  84.3 0.6 copy-start.6
  84.9 0.6 copy-start.7
  87.2 2.0 %copy-start.2 = (bf16[3,512,512]{2,1,0:T(8,128)(2,1)S(1)}, bf16[3,512,512]{2,1,0:T(8,128)(2,1)}, u32[]{:S(2)}) copy-start(bf16[3,512,512]{2,1,0:T(8,128)(2,1)} %get-tuple-element.31) | copy-start | bytes 4718596

commit v4 on v3

--- a/solution.py
+++ b/solution.py
@@ -17,7 +17,7 @@
 def attention_kernel(
     q_hbm, mem_in, wk_hbm, wv_hbm, g_hbm,
     att_hbm, gq_hbm, kvg_hbm, mem_hbm, gm0_hbm, gm1_hbm, gm2_hbm, gm3_hbm,
-    q_v, g_v, qt_v, gt_v, att_t, gq_t, w_v, mem_ref, mg, acc, kvt, part, own, landed, kvg,
+    q_v, g_v, qt_v, gt_v, att_t, gq_t, w_v, mem_ref, mg, mt, acc, kvt, part, own, landed, kvg,
     gm_v, gm_landed,
     in_sem, w_sem, out_sem, z_send, z_recv, d_send, d_recv, s_send, s_recv,
     rs_send, rs_recv, ag_send, ag_recv, gm_sem,
@@ -126,10 +126,13 @@
         qt_v[n // DP, lanes, :] = q_v[n // DP, :, lanes].T
         gt_v[n // DP, lanes, :] = g_v[n // DP, :, lanes].T
 
-    acc[...] = jnp.zeros_like(acc)
+    def columns(step):
+        return pl.ds(pl.multiple_of((i + DP - step) % DP * quarter, quarter), quarter)
+
+    def project(layer, kv, step):
+        return jnp.dot(w_v[layer, kv, :, columns(step)], mt[step], preferred_element_type=F32)
+
     for step in range(DP):
-        j = (i + DP - step) % DP
-        cols = pl.ds(pl.multiple_of(j * quarter, quarter), quarter)
         if step >= 1:
             d_copies[step - 1].wait_recv()
             s_copies.append(to_sibling(step))
@@ -137,20 +140,33 @@
         for copy in load_w(step):
             copy.wait()
         s_copies[step].wait_recv()
-
-        @pl.loop(0, layers * 2)
-        def project(n):
-            mem_cols = mg[j].reshape(mem_total, quarter)
-            acc[n // 2, n % 2] += lax.dot_general(
-                w_v[n // 2, n % 2, :, cols],
-                mem_cols,
-                (((1,), (1,)), ((), ())),
-                preferred_element_type=F32,
-            )
-
-    kvt[...] = acc[...].astype(BF16)
-    for copy in z_copies + d_copies + s_copies:
-        copy.wait_send()
+        mt[step] = mg[(i + DP - step) % DP].reshape(mem_total, quarter).T
+        if step == 0:
+
+            @pl.loop(0, layers * 2)
+            def first_quarter(n):
+                acc[n // 2, n % 2] = project(n // 2, n % 2, 0)
+
+        elif step < DP - 1:
+
+            @pl.loop(0, 2)
+            def layer_0(kv):
+                acc[0, kv] += project(0, kv, step)
+
+        else:
+
+            @pl.loop(0, 2)
+            def layer_0_last(kv):
+                kvt[0, kv] = (acc[0, kv] + project(0, kv, step)).astype(BF16)
+
+    def finish_projection(layer):
+        @pl.loop(0, 2)
+        def one(kv):
+            total = acc[layer, kv]
+            for step in range(1, DP):
+                total = total + project(layer, kv, step)
+            kvt[layer, kv] = total.astype(BF16)
+
     mem_out = pltpu.make_async_copy(mg, mem_hbm, out_sem.at[0])
     mem_out.start()
 
@@ -245,14 +261,14 @@
 
     @pl.loop(0, layers)
     def one_layer(layer):
+        @pl.when(layer >= 1)
+        def _():
+            finish_projection(layer)
+            reduce(layer - 1)
+
         first, second = attend(layer, 0), attend(layer, 1)
         send_part(layer, 0, first)
         send_part(layer, 1, second)
-
-        @pl.when(layer >= 1)
-        def _():
-            reduce(layer - 1)
-
         third, last = attend(layer, 2), attend(layer, 3)
         send_part(layer, 2, third)
         for kv in range(2):
@@ -277,14 +293,8 @@
         add_memory_gradient(layer)
     reduce(layers - 1)
 
-    @pl.loop(0, layers * DP)
-    def turn_back(n):
-        lanes = pair_rows(n % DP)
-        q_v[n // DP, :, lanes] = att_t[n // DP, lanes, :].T
-        g_v[n // DP, :, lanes] = gq_t[n // DP, lanes, :].T
-
-    att_out = pltpu.make_async_copy(q_v, att_hbm, out_sem.at[1])
-    gq_out = pltpu.make_async_copy(g_v, gq_hbm, out_sem.at[2])
+    att_out = pltpu.make_async_copy(att_t, att_hbm, out_sem.at[1])
+    gq_out = pltpu.make_async_copy(gq_t, gq_hbm, out_sem.at[2])
     att_out.start()
     gq_out.start()
     for layer in range(max(layers - 2, 0), layers):
@@ -300,6 +310,8 @@
         device_id_type=MESH,
     )
     gm_copy.start()
+    for copy in z_copies + d_copies + s_copies:
+        copy.wait_send()
     for layer in range(layers):
         for t in range(DP - 1):
             rs_copy(layer, t).wait_send()
@@ -324,8 +336,8 @@
     any_spec = pl.BlockSpec(memory_space=pl.ANY)
     dma = pltpu.SemaphoreType.DMA
     out_shape = (
-        jax.ShapeDtypeStruct(queries.shape, BF16),
-        jax.ShapeDtypeStruct(queries.shape, BF16),
+        jax.ShapeDtypeStruct((layers, width, rows), BF16),
+        jax.ShapeDtypeStruct((layers, width, rows), BF16),
         jax.ShapeDtypeStruct((layers, 2, width, mem_total), BF16),
         jax.ShapeDtypeStruct((DP, CORES, CHIPS, tokens, quarter), BF16),
     ) + (jax.ShapeDtypeStruct((tokens, quarter), F32),) * CHIPS
@@ -344,6 +356,7 @@
             pltpu.VMEM((layers, 2, width, model), BF16),
             pltpu.VMEM(memory.shape, BF16),
             pltpu.VMEM((DP, CORES, CHIPS, tokens, quarter), BF16),
+            pltpu.VMEM((DP, quarter, mem_total), BF16),
             pltpu.VMEM((layers, 2, width, mem_total), F32),
             pltpu.VMEM((layers, 2, width, mem_total), BF16),
             pltpu.VMEM((layers, DP - 1, 2, PAIR, mem_total), BF16),
@@ -377,36 +390,42 @@
     )(queries, memory, w_key, w_value, grad_out)
 
 
-def weight_kernel(kvg_ref, mem_ref, out_ref):
-    quarter = mem_ref.shape[-1]
-    for j in range(DP):
-        out_ref[0, :, j * quarter : (j + 1) * quarter] = jnp.dot(
-            kvg_ref[0, 0], mem_ref[j], preferred_element_type=F32
-        )
-
-
-def weight_gradient(kvg, mem, kv):
+def weight_kernel(kvg_ref, mem_ref, turned_ref, out_ref, back_ref):
+    out_ref[0] = jnp.dot(
+        kvg_ref[0, 0], mem_ref[pl.program_id(1)], preferred_element_type=F32
+    )
+    back_ref[0] = turned_ref[0].T
+
+
+def weight_gradient(kvg, mem, turned, kv):
     layers, _, width, mem_total = kvg.shape
     quarter = mem.shape[-1]
     model = DP * quarter
-    rows = 128
+    rows = turned.shape[-1]
     return pl.pallas_call(
         weight_kernel,
-        grid=(layers, width // rows),
+        grid=(layers, DP),
         in_specs=[
-            pl.BlockSpec((1, 1, rows, mem_total), lambda l, c: (l, kv, c, 0)),
-            pl.BlockSpec((DP, mem_total, quarter), lambda l, c: (0, 0, 0)),
+            pl.BlockSpec((1, 1, width, mem_total), lambda l, j: (l, kv, 0, 0)),
+            pl.BlockSpec((DP, mem_total, quarter), lambda l, j: (0, 0, 0)),
+            pl.BlockSpec((1, PAIR, rows), lambda l, j: (l, j, 0)),
         ],
-        out_specs=pl.BlockSpec((1, rows, model), lambda l, c: (l, c, 0)),
-        out_shape=jax.ShapeDtypeStruct((layers, width, model), F32),
+        out_specs=[
+            pl.BlockSpec((1, width, quarter), lambda l, j: (l, 0, j)),
+            pl.BlockSpec((1, rows, PAIR), lambda l, j: (l, 0, j)),
+        ],
+        out_shape=(
+            jax.ShapeDtypeStruct((layers, width, model), F32),
+            jax.ShapeDtypeStruct((layers, rows, width), BF16),
+        ),
         compiler_params=pltpu.CompilerParams(vmem_limit_bytes=32 * 2**20),
         cost_estimate=pl.CostEstimate(
             flops=2 * layers * width * mem_total * model,
-            bytes_accessed=4 * layers * width * model,
+            bytes_accessed=4 * layers * width * (model + rows),
             transcendentals=0,
         ),
         name=("grad_w_key", "grad_w_value")[kv],
-    )(kvg, mem)
+    )(kvg, mem, turned)
 
 
 def place_kernel(*refs):
@@ -419,7 +438,7 @@
 
 
 def fused_shards(queries, memory, w_key, w_value, grad_out):
-    attended, grad_queries, kvg, mem, *gm_parts = attention(
+    attended_t, grad_queries_t, kvg, mem, *gm_parts = attention(
         queries, memory, w_key, w_value, grad_out
     )
     tokens, model = memory.shape
@@ -432,12 +451,12 @@
             for core in range(CORES)
         ]
         gm = gm + lax.ppermute(gm_parts[k], "mp", ring)
-    grad_w_key = weight_gradient(kvg, mem, 0)
+    grad_w_key, attended = weight_gradient(kvg, mem, attended_t, 0)
     grad_w_key, gm = lax.optimization_barrier((grad_w_key, gm))
     quarters = [gm] + [
         lax.ppermute(gm, "dp", [(i, (i + k) % DP) for i in range(DP)]) for k in range(1, DP)
     ]
-    grad_w_value = weight_gradient(kvg, mem, 1)
+    grad_w_value, grad_queries = weight_gradient(kvg, mem, grad_queries_t, 1)
     grad_memory = pl.pallas_call(
         place_kernel,
         in_specs=[pl.BlockSpec(memory_space=pltpu.VMEM)] * DP,

time: 90.6 us -> 87 us (0.960)
  Pallas kernels: 75.5 us -> 73.2 us
  local copies, waits for them, and re-layouts: 6.5 us -> 4.76 us
    pallas_call x1, Pallas kernels: 51.6 us -> 49.2 us  [attention(): pl.pallas_call(attention_kernel, out_shape=out_shape, in_specs=[any_spec,...]
    unnamed x18 -> x16, local copies, waits for them, and re-layouts: 6.5 us -> 4.76 us
  transfers between devices with their start and end apart: 6 -> 6, of which waited for: 0 -> 0; matrix products, arithmetic and copies ran while one was open for 0% -> 0% of each run, Pallas kernels for 25% -> 26%
where the time goes in v4:
time: 87 us; the launch traced here: 86.7 us
  Pallas kernels  73.2 us (84%)
  starting transfers between devices  7.98 us (9%)
  local copies, waits for them, and re-layouts  4.76 us (5%)
    pallas_call x1, Pallas kernels, attention(): pl.pallas_call(attention_kernel, out_shape=out_shape, in_specs=[any_spec,...  49.2 us
    pallas_call x2, Pallas kernels, weight_gradient(): pl.pallas_call(weight_kernel, grid=(layers, DP), in_specs=[pl.BlockSpec((...  22.3 us
    ppermute x3, starting transfers between devices, fused_shards(): gm = gm + lax.ppermute(gm_parts[k], 'mp', ring)  4.79 us
    unnamed x16, local copies, waits for them, and re-layouts  4.76 us
    ppermute x3, starting transfers between devices, fused_shards(): lax.ppermute(gm, 'dp', [(i, (i + k) % DP) for i in range(DP)])  3.19 us
  transfers between devices with their start and end apart: 6, of which 0 were waited for; matrix products, arithmetic and copies ran while one was open for 0% of the time, Pallas kernels for 26%

profile of v4, /device:TPU:0, one launch (start us, length us, event | category | flops | bytes accessed | tf_op | source)
XLA Modules:
  0.0 86.7 jit_solution(5599474644853787602)
XLA Ops:
  0.6 0.0 copy-start
  0.6 0.9 %copy-done = bf16[16,4096]{1,0:T(8,128)(2,1)S(1)} copy-done((bf16[16,4096]{1,0:T(8,128)(2,1)S(1)}, bf16[16,4096]{1,0:T(8,128)(2,1)}, u32[]{:S(2)}) %copy-start) | copy-done | bytes 131096
  1.5 49.2 %attention.1 = (bf16[3,512,512]{2,1,0:T(8,128)(2,1)}, bf16[3,512,512]{2,1,0:T(8,128)(2,1)}, bf16[3,2,512,128]{3,2,1,0:T(8,128)(2,1)S(1)}, bf16[4,2,4,16,1024]{4,...) custom-call(bf16[3,512,512]{2,1,0:T(8,128)(2,1)} %q_hbm.1, ...), custom_call_target="tpu_custom_call" | custom-call | flops 8000000000 | bytes 35000000 | tf_op jit(solution)/shard_map/attention/pallas_call | solution.py:344
  50.8 1.4 %collective-permute-start = (f32[16,1024]{1,0:T(8,128)S(1)}, f32[16,1024]{1,0:T(8,128)S(1)}, u32[]{:S(2)}, u32[]{:S(2)}) collective-permute-start(f32[16,1024]{1,0:T(8,128)S(1)} %get-tuple-element.27), channel_id=1, source_target_pairs={{0,2},{1,3},{2,4},{3,5},{4,6},{5,7},{6,0},{7,1},{8,10},{9,11},{10,... | collective-permute-start | bytes 196616 | tf_op jit(solution)/shard_map/ppermute | solution.py:453
  52.2 2.3 %collective-permute-start.1 = (f32[16,1024]{1,0:T(8,128)S(1)}, f32[16,1024]{1,0:T(8,128)S(1)}, u32[]{:S(2)}, u32[]{:S(2)}) collective-permute-start(f32[16,1024]{1,0:T(8,128)S(1)} %get-tuple-element.28), channel_id=1, source_target_pairs={{0,4},{1,5},{2,6},{3,7},{4,0},{5,1},{6,2},{7,3},{8,12},{9,13},{10,... | collective-permute-start | bytes 196616 | tf_op jit(solution)/shard_map/ppermute | solution.py:453
  54.5 1.1 %collective-permute-start.2 = (f32[16,1024]{1,0:T(8,128)S(1)}, f32[16,1024]{1,0:T(8,128)S(1)}, u32[]{:S(2)}, u32[]{:S(2)}) collective-permute-start(f32[16,1024]{1,0:T(8,128)S(1)} %get-tuple-element.29), channel_id=1, source_target_pairs={{0,6},{1,7},{2,0},{3,1},{4,2},{5,3},{6,4},{7,5},{8,14},{9,15},{10,... | collective-permute-start | bytes 196616 | tf_op jit(solution)/shard_map/ppermute | solution.py:453
  55.6 0.0 copy-start.1
  55.6 1.2 %copy-done.1 = bf16[4,2,4,16,1024]{4,3,2,1,0:T(8,128)(2,1)S(1)} copy-done((bf16[4,2,4,16,1024]{4,3,2,1,0:T(8,128)(2,1)S(1)}, bf16[4,2,4,16,1024]{4,3,2,1,0:T(8,128)(2,1)}, u32[]{:S(2)}) %copy-start.1) | copy-done | bytes 1048600
  56.8 0.0 copy-start.3
  56.8 1.4 %copy-done.3 = bf16[3,512,512]{2,1,0:T(8,128)(2,1)S(1)} copy-done((bf16[3,512,512]{2,1,0:T(8,128)(2,1)S(1)}, bf16[3,512,512]{2,1,0:T(8,128)(2,1)}, u32[]{:S(2)}) %copy-start.3) | copy-done | bytes 1572888
  58.2 0.0 copy-start.2
  58.2 11.2 %grad_w_key.1 = (f32[3,512,4096]{2,1,0:T(8,128)}, bf16[3,512,512]{2,1,0:T(8,128)(2,1)}) custom-call(bf16[3,2,512,128]{3,2,1,0:T(8,128)(2,1)S(1)} %get-tuple-element.19.kvg_ref, bf16[4,128,1024]{2,1,0:T(8,128)(2,1)S(1)} %bitcast.1, bf16[3,512,512]{2,1,0:T(8,128)(2,1)S(1)} %copy-done.3), custom_call_target="tpu_custom_call" | custom-call | flops 1610612736 | bytes 28311552 | tf_op jit(solution)/shard_map/grad_w_key/pallas_call | solution.py:405
  69.4 0.0 collective-permute-done
  69.4 0.0 collective-permute-done.1
  69.4 0.0 collective-permute-done.2
  69.4 0.0 copy-start.4
  69.4 2.1 %collective-permute-start.5 = (f32[16,1024]{1,0:T(8,128)S(1)}, f32[16,1024]{1,0:T(8,128)S(1)}, u32[]{:S(2)}, u32[]{:S(2)}) collective-permute-start(f32[16,1024]{1,0:T(8,128)S(1)} %add_add_fusion.refs_0_), channel_id=1, source_target_pairs={{0,24},{8,0},{16,8},{24,16},{1,25},{9,1},{17,9},{25,17},{2,26},{10... | collective-permute-start | bytes 196616 | tf_op jit(solution)/shard_map/ppermute | solution.py:457
  71.5 0.0 collective-permute-start.4
  71.5 1.1 %collective-permute-start.3 = (f32[16,1024]{1,0:T(8,128)S(1)}, f32[16,1024]{1,0:T(8,128)S(1)}, u32[]{:S(2)}, u32[]{:S(2)}) collective-permute-start(f32[16,1024]{1,0:T(8,128)S(1)} %add_add_fusion.refs_0_), channel_id=1, source_target_pairs={{0,8},{8,16},{16,24},{24,0},{1,9},{9,17},{17,25},{25,1},{2,10},{10... | collective-permute-start | bytes 196616 | tf_op jit(solution)/shard_map/ppermute | solution.py:457
  72.6 0.0 copy-done.2
  72.6 11.2 %grad_w_value.1 = (f32[3,512,4096]{2,1,0:T(8,128)}, bf16[3,512,512]{2,1,0:T(8,128)(2,1)}) custom-call(bf16[3,2,512,128]{3,2,1,0:T(8,128)(2,1)S(1)} %get-tuple-element.19.kvg_ref, bf16[4,128,1024]{2,1,0:T(8,128)(2,1)S(1)} %bitcast.2, bf16[3,512,512]{2,1,0:T(8,128)(2,1)S(1)} %copy-done.2), custom_call_target="tpu_custom_call" | custom-call | flops 1610612736 | bytes 28311552 | tf_op jit(solution)/shard_map/grad_w_value/pallas_call | solution.py:405
  83.8 0.0 copy-done.4
  83.8 0.0 collective-permute-done.5.refs_3_
  83.8 0.0 copy-start.5
  83.8 0.0 collective-permute-done.4.refs_2_
  83.8 0.0 copy-start.6
  83.8 0.0 collective-permute-done.3.refs_1_
  83.8 0.6 copy-done.5
  84.4 0.0 copy-done.6
  84.4 0.0 copy-start.7
  84.4 0.6 copy-done.7
  85.1 1.7 %place.1 = f32[16,4096]{1,0:T(8,128)} custom-call(f32[16,1024]{1,0:T(8,128)} %copy-done.4, f32[16,1024]{1,0:T(8,128)} %copy-done.7, f32[16,1024]{1,0:T(8,128)} %copy-done.6, f32[16,1024]{1,0:T(8,128)} %copy-done.5), custom_call_target="tpu_custom_call" | custom-call | tf_op jit(solution)/shard_map/place/pallas_call | solution.py:460
  (1 shorter events, 0.0 us)
Async XLA Ops:
  0.6 0.9 %copy-start = (bf16[16,4096]{1,0:T(8,128)(2,1)S(1)}, bf16[16,4096]{1,0:T(8,128)(2,1)}, u32[]{:S(2)}) copy-start(bf16[16,4096]{1,0:T(8,128)(2,1)} %mem_in.1) | copy-start | bytes 393220
  50.8 18.6 %collective-permute-start = (f32[16,1024]{1,0:T(8,128)S(1)}, f32[16,1024]{1,0:T(8,128)S(1)}, u32[]{:S(2)}, u32[]{:S(2)}) collective-permute-start(f32[16,1024]{1,0:T(8,128)S(1)} %get-tuple-element.27), channel_id=1, source_target_pairs={{0,2},{1,3},{2,4},{3,5},{4,6},{5,7},{6,0},{7,1},{8,10},{9,11},{10,... | collective-permute-start | bytes 196616 | tf_op jit(solution)/shard_map/ppermute | solution.py:453
  52.2 17.2 %collective-permute-start.1 = (f32[16,1024]{1,0:T(8,128)S(1)}, f32[16,1024]{1,0:T(8,128)S(1)}, u32[]{:S(2)}, u32[]{:S(2)}) collective-permute-start(f32[16,1024]{1,0:T(8,128)S(1)} %get-tuple-element.28), channel_id=1, source_target_pairs={{0,4},{1,5},{2,6},{3,7},{4,0},{5,1},{6,2},{7,3},{8,12},{9,13},{10,... | collective-permute-start | bytes 196616 | tf_op jit(solution)/shard_map/ppermute | solution.py:453
  54.5 14.9 %collective-permute-start.2 = (f32[16,1024]{1,0:T(8,128)S(1)}, f32[16,1024]{1,0:T(8,128)S(1)}, u32[]{:S(2)}, u32[]{:S(2)}) collective-permute-start(f32[16,1024]{1,0:T(8,128)S(1)} %get-tuple-element.29), channel_id=1, source_target_pairs={{0,6},{1,7},{2,0},{3,1},{4,2},{5,3},{6,4},{7,5},{8,14},{9,15},{10,... | collective-permute-start | bytes 196616 | tf_op jit(solution)/shard_map/ppermute | solution.py:453
  55.6 1.2 %copy-start.1 = (bf16[4,2,4,16,1024]{4,3,2,1,0:T(8,128)(2,1)S(1)}, bf16[4,2,4,16,1024]{4,3,2,1,0:T(8,128)(2,1)}, u32[]{:S(2)}) copy-start(bf16[4,2,4,16,1024]{4,3,2,1,0:T(8,128)(2,1)} %get-tuple-element.20) | copy-start | bytes 3145732
  56.8 1.4 %copy-start.3 = (bf16[3,512,512]{2,1,0:T(8,128)(2,1)S(1)}, bf16[3,512,512]{2,1,0:T(8,128)(2,1)}, u32[]{:S(2)}) copy-start(bf16[3,512,512]{2,1,0:T(8,128)(2,1)} %get-tuple-element.21.turned_ref) | copy-start | bytes 4718596
  58.2 14.4 %copy-start.2 = (bf16[3,512,512]{2,1,0:T(8,128)(2,1)S(1)}, bf16[3,512,512]{2,1,0:T(8,128)(2,1)}, u32[]{:S(2)}) copy-start(bf16[3,512,512]{2,1,0:T(8,128)(2,1)} %get-tuple-element.23.turned_ref) | copy-start | bytes 4718596
  69.4 14.4 %copy-start.4 = (f32[16,1024]{1,0:T(8,128)}, f32[16,1024]{1,0:T(8,128)S(1)}, u32[]{:S(2)}) copy-start(f32[16,1024]{1,0:T(8,128)S(1)} %add_add_fusion.refs_0_) | copy-start | bytes 196612
  69.4 14.4 %collective-permute-start.5 = (f32[16,1024]{1,0:T(8,128)S(1)}, f32[16,1024]{1,0:T(8,128)S(1)}, u32[]{:S(2)}, u32[]{:S(2)}) collective-permute-start(f32[16,1024]{1,0:T(8,128)S(1)} %add_add_fusion.refs_0_), channel_id=1, source_target_pairs={{0,24},{8,0},{16,8},{24,16},{1,25},{9,1},{17,9},{25,17},{2,26},{10... | collective-permute-start | bytes 196616 | tf_op jit(solution)/shard_map/ppermute | solution.py:457
  71.5 12.3 %collective-permute-start.4 = (f32[16,1024]{1,0:T(8,128)S(1)}, f32[16,1024]{1,0:T(8,128)S(1)}, u32[]{:S(2)}, u32[]{:S(2)}) collective-permute-start(f32[16,1024]{1,0:T(8,128)S(1)} %add_add_fusion.refs_0_), channel_id=1, source_target_pairs={{0,16},{8,24},{16,0},{24,8},{1,17},{9,25},{17,1},{25,9},{2,18},{10... | collective-permute-start | bytes 196616 | tf_op jit(solution)/shard_map/ppermute | solution.py:457
  71.5 12.3 %collective-permute-start.3 = (f32[16,1024]{1,0:T(8,128)S(1)}, f32[16,1024]{1,0:T(8,128)S(1)}, u32[]{:S(2)}, u32[]{:S(2)}) collective-permute-start(f32[16,1024]{1,0:T(8,128)S(1)} %add_add_fusion.refs_0_), channel_id=1, source_target_pairs={{0,8},{8,16},{16,24},{24,0},{1,9},{9,17},{17,25},{25,1},{2,10},{10... | collective-permute-start | bytes 196616 | tf_op jit(solution)/shard_map/ppermute | solution.py:457
  83.8 0.6 copy-start.5
  83.8 0.6 copy-start.6
  84.4 0.6 copy-start.7

commit v5 on v4

--- a/solution.py
+++ b/solution.py
@@ -1,3 +1,5 @@
+import functools
+
 import jax
 import jax.numpy as jnp
 from jax import lax
@@ -17,7 +19,7 @@
 def attention_kernel(
     q_hbm, mem_in, wk_hbm, wv_hbm, g_hbm,
     att_hbm, gq_hbm, kvg_hbm, mem_hbm, gm0_hbm, gm1_hbm, gm2_hbm, gm3_hbm,
-    q_v, g_v, qt_v, gt_v, att_t, gq_t, w_v, mem_ref, mg, mt, acc, kvt, part, own, landed, kvg,
+    q_v, g_v, qt_v, gt_v, att_t, gq_t, w_v, mem_ref, mg, mt, acc, kvt, part, own, hold, landed, kvg,
     gm_v, gm_landed,
     in_sem, w_sem, out_sem, z_send, z_recv, d_send, d_recv, s_send, s_recv,
     rs_send, rs_recv, ag_send, ag_recv, gm_sem,
@@ -35,14 +37,18 @@
     def z_peer(k):
         return {"dp": i, "mp": ((z + k) % CHIPS) * CORES + core}
 
-    def d_peer(k):
-        return {"dp": (i + k) % DP, "mp": me}
+    x, y = i % 2, i // 2
+    i_x, i_y, i_far = y * 2 + 1 - x, (1 - y) * 2 + x, DP - 1 - i
+    order = (i, i_x, i_y, i_far)
+    to_x, to_y = {"dp": i_x, "mp": me}, {"dp": i_y, "mp": me}
 
     sib = {"dp": i, "mp": sibling}
 
+    def columns(step):
+        return pl.ds(pl.multiple_of(order[step] * quarter, quarter), quarter)
+
     def load_w(step):
-        j = (i + DP - step) % DP
-        cols = pl.ds(pl.multiple_of(j * quarter, quarter), quarter)
+        cols = columns(step)
         return [
             pltpu.make_async_copy(
                 hbm.at[:, :, cols], w_v.at[:, kv, :, cols], w_sem.at[step, kv]
@@ -63,13 +69,12 @@
     barrier = pltpu.get_barrier_semaphore()
     for k in range(1, CHIPS):
         pl.semaphore_signal(barrier, inc=1, device_id=z_peer(k), device_id_type=MESH)
-    for k in range(1, DP):
-        pl.semaphore_signal(barrier, inc=1, device_id=d_peer(k), device_id_type=MESH)
-    pl.semaphore_signal(barrier, inc=1, device_id=sib, device_id_type=MESH)
+    for peer in (to_x, to_y, sib):
+        pl.semaphore_signal(barrier, inc=1, device_id=peer, device_id_type=MESH)
     load_mem.wait()
-    pl.semaphore_wait(barrier, CHIPS + DP - 1)
-
-    mine = pl.ds(pl.multiple_of(i * quarter, quarter), quarter)
+    pl.semaphore_wait(barrier, CHIPS - 1 + 3)
+
+    mine = columns(0)
     z_copies = []
     for k in range(1, CHIPS):
         z_copies.append(
@@ -88,31 +93,37 @@
         copy.wait_recv()
 
     def to_sibling(step):
-        j = (i + DP - step) % DP
+        block = mg.at[order[step], core]
         return pltpu.make_async_remote_copy(
-            src_ref=mg.at[j, core],
-            dst_ref=mg.at[j, core],
+            src_ref=block,
+            dst_ref=block,
             send_sem=s_send.at[step],
             recv_sem=s_recv.at[step],
             device_id=sib,
             device_id_type=MESH,
         )
 
-    d_copies = []
-    s_copies = [to_sibling(0)]
+    def gather_copy(block, at, peer):
+        return pltpu.make_async_remote_copy(
+            src_ref=block,
+            dst_ref=block,
+            send_sem=d_send.at[at],
+            recv_sem=d_recv.at[at],
+            device_id=peer,
+            device_id_type=MESH,
+        )
+
+    half = CHIPS // 2
+    s_copies = [to_sibling(step) for step in range(DP)]
+    d_copies = [
+        gather_copy(mg.at[i, core], 0, to_x),
+        gather_copy(mg.at[i, core], 1, to_y),
+        gather_copy(mg.at[i_x, core, pl.ds(0, half)], 2, to_y),
+        gather_copy(mg.at[i_y, core, pl.ds(half, half)], 3, to_x),
+    ]
+    d_copies[0].start()
+    d_copies[1].start()
     s_copies[0].start()
-    for k in range(1, DP):
-        d_copies.append(
-            pltpu.make_async_remote_copy(
-                src_ref=mg.at[i, core],
-                dst_ref=mg.at[i, core],
-                send_sem=d_send.at[k - 1],
-                recv_sem=d_recv.at[k - 1],
-                device_id=d_peer(k),
-                device_id_type=MESH,
-            )
-        )
-        d_copies[-1].start()
 
     def pair_rows(pair):
         return pl.ds(pl.multiple_of(pair * PAIR, PAIR), PAIR)
@@ -126,21 +137,23 @@
         qt_v[n // DP, lanes, :] = q_v[n // DP, :, lanes].T
         gt_v[n // DP, lanes, :] = g_v[n // DP, :, lanes].T
 
-    def columns(step):
-        return pl.ds(pl.multiple_of((i + DP - step) % DP * quarter, quarter), quarter)
-
     def project(layer, kv, step):
         return jnp.dot(w_v[layer, kv, :, columns(step)], mt[step], preferred_element_type=F32)
 
     for step in range(DP):
-        if step >= 1:
-            d_copies[step - 1].wait_recv()
-            s_copies.append(to_sibling(step))
-            s_copies[step].start()
+        if step == 1:
+            for near in range(2):
+                d_copies[near].wait_recv()
+                d_copies[2 + near].start()
+                s_copies[1 + near].start()
+        elif step == 3:
+            d_copies[2].wait_recv()
+            d_copies[3].wait_recv()
+            s_copies[3].start()
         for copy in load_w(step):
             copy.wait()
         s_copies[step].wait_recv()
-        mt[step] = mg[(i + DP - step) % DP].reshape(mem_total, quarter).T
+        mt[step] = mg[order[step]].reshape(mem_total, quarter).T
         if step == 0:
 
             @pl.loop(0, layers * 2)
@@ -170,35 +183,52 @@
     mem_out = pltpu.make_async_copy(mg, mem_hbm, out_sem.at[0])
     mem_out.start()
 
-    def rs_copy(layer, t):
+    def rs_copy(layer, slot):
         return pltpu.make_async_remote_copy(
-            src_ref=part.at[layer, t],
-            dst_ref=landed.at[layer, t],
-            send_sem=rs_send.at[layer, t],
-            recv_sem=rs_recv.at[layer, t],
-            device_id={"dp": (i + 1 + t) % DP, "mp": me},
+            src_ref=part.at[layer, slot],
+            dst_ref=landed.at[layer, slot],
+            send_sem=rs_send.at[layer, slot],
+            recv_sem=rs_recv.at[layer, slot],
+            device_id=to_x if slot % 2 == 0 else to_y,
             device_id_type=MESH,
         )
 
-    def ag_copy(layer, k):
-        block = kvg.at[layer, :, pair_rows(i), :]
+    def send_part(layer, slot, term):
+        part[layer, slot] = term.astype(BF16)
+        rs_copy(layer, slot).start()
+
+    def came(layer, slot):
+        rs_copy(layer, slot).wait_recv()
+        return landed[layer, slot].astype(F32)
+
+    def ag_copy(layer, at):
+        block = (
+            kvg.at[layer, :, pair_rows(i), :],
+            kvg.at[layer, :, pair_rows(i), :],
+            kvg.at[layer, 0, pair_rows(i_x), :],
+            kvg.at[layer, 1, pair_rows(i_y), :],
+        )[at]
         return pltpu.make_async_remote_copy(
             src_ref=block,
             dst_ref=block,
-            send_sem=ag_send.at[layer, k - 1],
-            recv_sem=ag_recv.at[layer, k - 1],
-            device_id=d_peer(k),
+            send_sem=ag_send.at[layer, at],
+            recv_sem=ag_recv.at[layer, at],
+            device_id=(to_x, to_y, to_y, to_x)[at],
             device_id_type=MESH,
         )
 
     def reduce(layer):
-        total = own[layer]
-        for t in range(DP - 1):
-            rs_copy(layer, t).wait_recv()
-            total = total + landed[layer, t].astype(F32)
-        kvg[layer, :, pair_rows(i), :] = total.astype(BF16)
-        for k in range(1, DP):
-            ag_copy(layer, k).start()
+        keys = own[layer, 0] + came(layer, 2) + came(layer, 5)
+        values = own[layer, 1] + came(layer, 3) + came(layer, 4)
+        kvg[layer, 0, pair_rows(i), :] = keys.astype(BF16)
+        kvg[layer, 1, pair_rows(i), :] = values.astype(BF16)
+        ag_copy(layer, 0).start()
+        ag_copy(layer, 1).start()
+
+    def pass_on(layer):
+        for near in range(2):
+            ag_copy(layer, near).wait_recv()
+            ag_copy(layer, 2 + near).start()
 
     def head_masks(axis):
         return lax.broadcasted_iota(jnp.int32, (PAIR, PAIR), axis) < HEAD_WIDTH
@@ -217,8 +247,8 @@
     def dot_nt(lhs, rhs):
         return lax.dot_general(lhs, rhs, (((1,), (1,)), ((), ())), preferred_element_type=F32)
 
-    def attend(layer, t):
-        lanes = pair_rows((i + 1 + t) % DP)
+    def attend(layer, pair):
+        lanes = pair_rows(pair)
         queries, grads = qt_v[layer, lanes, :], gt_v[layer, lanes, :]
         keys, values = kvt[layer, 0, lanes, :], kvt[layer, 1, lanes, :]
         scores = jnp.dot(
@@ -254,11 +284,6 @@
         ).astype(BF16)
         return own_blocks(dot_nt(queries, grad_scores)), own_blocks(dot_nt(grads, probs_b))
 
-    def send_part(layer, t, grads):
-        for kv in range(2):
-            part[layer, t, kv] = grads[kv].astype(BF16)
-        rs_copy(layer, t).start()
-
     @pl.loop(0, layers)
     def one_layer(layer):
         @pl.when(layer >= 1)
@@ -266,17 +291,26 @@
             finish_projection(layer)
             reduce(layer - 1)
 
-        first, second = attend(layer, 0), attend(layer, 1)
-        send_part(layer, 0, first)
-        send_part(layer, 1, second)
-        third, last = attend(layer, 2), attend(layer, 3)
-        send_part(layer, 2, third)
+        far, by_x = attend(layer, i_far), attend(layer, i_x)
+        send_part(layer, 0, far[0])
+        send_part(layer, 1, far[1])
+        send_part(layer, 2, by_x[0])
+        hold[0] = by_x[1]
+        by_y, mine_both = attend(layer, i_y), attend(layer, i)
+        send_part(layer, 3, by_y[1])
+        hold[1] = by_y[0]
         for kv in range(2):
-            own[layer, kv] = last[kv]
+            own[layer, kv] = mine_both[kv]
+        send_part(layer, 4, hold[0] + came(layer, 1))
+        send_part(layer, 5, hold[1] + came(layer, 0))
+
+        @pl.when(layer >= 1)
+        def _():
+            pass_on(layer - 1)
 
     def add_memory_gradient(layer):
-        for k in range(1, DP):
-            ag_copy(layer, k).wait_recv()
+        for at in (2, 3):
+            ag_copy(layer, at).wait_recv()
         for kv in range(2):
             term = lax.dot_general(
                 kvg[layer, kv],
@@ -289,15 +323,15 @@
             else:
                 gm_v[...] += term
 
-    for layer in range(layers - 2):
-        add_memory_gradient(layer)
     reduce(layers - 1)
 
     att_out = pltpu.make_async_copy(att_t, att_hbm, out_sem.at[1])
     gq_out = pltpu.make_async_copy(gq_t, gq_hbm, out_sem.at[2])
     att_out.start()
     gq_out.start()
-    for layer in range(max(layers - 2, 0), layers):
+    for layer in range(layers):
+        if layer == layers - 1:
+            pass_on(layer)
         add_memory_gradient(layer)
     kvg_out = pltpu.make_async_copy(kvg, kvg_hbm, out_sem.at[3])
     kvg_out.start()
@@ -313,9 +347,10 @@
     for copy in z_copies + d_copies + s_copies:
         copy.wait_send()
     for layer in range(layers):
-        for t in range(DP - 1):
-            rs_copy(layer, t).wait_send()
-            ag_copy(layer, t + 1).wait_send()
+        for slot in range(6):
+            rs_copy(layer, slot).wait_send()
+        for at in range(4):
+            ag_copy(layer, at).wait_send()
     gm_copy.wait()
     gm_landed[...] += gm_v[core]
     gm_outs = [
@@ -359,9 +394,10 @@
             pltpu.VMEM((DP, quarter, mem_total), BF16),
             pltpu.VMEM((layers, 2, width, mem_total), F32),
             pltpu.VMEM((layers, 2, width, mem_total), BF16),
-            pltpu.VMEM((layers, DP - 1, 2, PAIR, mem_total), BF16),
+            pltpu.VMEM((layers, 6, PAIR, mem_total), BF16),
             pltpu.VMEM((layers, 2, PAIR, mem_total), F32),
-            pltpu.VMEM((layers, DP - 1, 2, PAIR, mem_total), BF16),
+            pltpu.VMEM((2, PAIR, mem_total), F32),
+            pltpu.VMEM((layers, 6, PAIR, mem_total), BF16),
             pltpu.VMEM((layers, 2, width, mem_total), BF16),
             pltpu.VMEM((CORES, CHIPS, tokens, quarter), F32),
             pltpu.VMEM((CHIPS, tokens, quarter), F32),
@@ -370,18 +406,18 @@
             dma((4 + CHIPS,)),
             dma((CHIPS - 1,)),
             dma((CHIPS - 1,)),
-            dma((DP - 1,)),
-            dma((DP - 1,)),
+            dma((4,)),
+            dma((4,)),
             dma((DP,)),
             dma((DP,)),
-            dma((layers, DP - 1)),
-            dma((layers, DP - 1)),
-            dma((layers, DP - 1)),
-            dma((layers, DP - 1)),
+            dma((layers, 6)),
+            dma((layers, 6)),
+            dma((layers, 4)),
+            dma((layers, 4)),
             dma((2,)),
         ],
         compiler_params=pltpu.CompilerParams(
-            collective_id=0, has_side_effects=True, vmem_limit_bytes=52 * 2**20
+            collective_id=0, has_side_effects=True, vmem_limit_bytes=60 * 2**20
         ),
         cost_estimate=pl.CostEstimate(
             flops=8 * 10**9, bytes_accessed=35 * 10**6, transcendentals=2 * 10**6
@@ -390,11 +426,61 @@
     )(queries, memory, w_key, w_value, grad_out)
 
 
-def weight_kernel(kvg_ref, mem_ref, turned_ref, out_ref, back_ref):
-    out_ref[0] = jnp.dot(
-        kvg_ref[0, 0], mem_ref[pl.program_id(1)], preferred_element_type=F32
-    )
-    back_ref[0] = turned_ref[0].T
+def weight_kernel(
+    kv, kvg_hbm, mem_hbm, turned_hbm, out_hbm, back_hbm,
+    kvg_v, mem_v, turned_v, ring, back_v, in_sem, ring_sem, back_sem,
+):
+    layers, width, _ = kvg_v.shape
+    quarter = mem_v.shape[-1]
+    slots = ring.shape[0]
+    loads = [
+        pltpu.make_async_copy(kvg_hbm.at[:, kv], kvg_v, in_sem.at[0]),
+        pltpu.make_async_copy(mem_hbm, mem_v, in_sem.at[1]),
+        pltpu.make_async_copy(turned_hbm, turned_v, in_sem.at[2]),
+    ]
+    for copy in loads:
+        copy.start()
+    loads[0].wait()
+    loads[1].wait()
+
+    def write(n):
+        at = pl.ds(pl.multiple_of(n % DP * PAIR, PAIR), PAIR)
+        return pltpu.make_async_copy(
+            ring.at[n % slots], out_hbm.at[n // DP, at, :], ring_sem.at[n % slots]
+        )
+
+    def write_back(layer):
+        return pltpu.make_async_copy(back_v.at[layer], back_hbm.at[layer], back_sem.at[layer])
+
+    @pl.loop(0, layers * DP)
+    def step(n):
+        layer = n // DP
+        at = pl.ds(pl.multiple_of(n % DP * PAIR, PAIR), PAIR)
+
+        @pl.when(n >= slots)
+        def _():
+            write(n - slots).wait()
+
+        for j in range(DP):
+            ring[n % slots, :, j * quarter : (j + 1) * quarter] = jnp.dot(
+                kvg_v[layer, at, :], mem_v[j], preferred_element_type=F32
+            )
+        write(n).start()
+
+        @pl.when(n == 0)
+        def _():
+            loads[2].wait()
+
+        back_v[layer, :, at] = turned_v[layer, at, :].T
+
+        @pl.when(n % DP == DP - 1)
+        def _():
+            write_back(layer).start()
+
+    for n in range(layers * DP - slots, layers * DP):
+        write(n).wait()
+    for layer in range(layers):
+        write_back(layer).wait()
 
 
 def weight_gradient(kvg, mem, turned, kv):
@@ -402,23 +488,28 @@
     quarter = mem.shape[-1]
     model = DP * quarter
     rows = turned.shape[-1]
+    slots = 4
+    any_spec = pl.BlockSpec(memory_space=pl.ANY)
+    dma = pltpu.SemaphoreType.DMA
     return pl.pallas_call(
-        weight_kernel,
-        grid=(layers, DP),
-        in_specs=[
-            pl.BlockSpec((1, 1, width, mem_total), lambda l, j: (l, kv, 0, 0)),
-            pl.BlockSpec((DP, mem_total, quarter), lambda l, j: (0, 0, 0)),
-            pl.BlockSpec((1, PAIR, rows), lambda l, j: (l, j, 0)),
-        ],
-        out_specs=[
-            pl.BlockSpec((1, width, quarter), lambda l, j: (l, 0, j)),
-            pl.BlockSpec((1, rows, PAIR), lambda l, j: (l, 0, j)),
-        ],
+        functools.partial(weight_kernel, kv),
+        in_specs=[any_spec] * 3,
+        out_specs=[any_spec] * 2,
         out_shape=(
             jax.ShapeDtypeStruct((layers, width, model), F32),
             jax.ShapeDtypeStruct((layers, rows, width), BF16),
         ),
-        compiler_params=pltpu.CompilerParams(vmem_limit_bytes=32 * 2**20),
+        scratch_shapes=[
+            pltpu.VMEM((layers, width, mem_total), BF16),
+            pltpu.VMEM(mem.shape, BF16),
+            pltpu.VMEM(turned.shape, BF16),
+            pltpu.VMEM((slots, PAIR, model), F32),
+            pltpu.VMEM((layers, rows, width), BF16),
+            dma((3,)),
+            dma((slots,)),
+            dma((layers,)),
+        ],
+        compiler_params=pltpu.CompilerParams(vmem_limit_bytes=60 * 2**20),
         cost_estimate=pl.CostEstimate(
             flops=2 * layers * width * mem_total * model,
             bytes_accessed=4 * layers * width * (model + rows),

time: 87 us -> 83.5 us (0.960)
  local copies, waits for them, and re-layouts: 4.76 us -> 1.25 us
    unnamed x16 -> x10, local copies, waits for them, and re-layouts: 4.76 us -> 1.25 us
    pallas_call x1, Pallas kernels: 49.2 us -> 50.4 us  [attention(): pl.pallas_call(attention_kernel, out_shape=out_shape, in_specs=[any_spec,...]
    pallas_call x2, Pallas kernels: 22.3 us -> 21.3 us  [weight_gradient(): pl.pallas_call(functools.partial(weight_kernel, kv), in_specs=[any_spec]...]
where the time goes in v5:
time: 83.5 us; the launch traced here: 83.2 us
  Pallas kernels  73.4 us (88%)
  starting transfers between devices  7.83 us (9%)
  local copies, waits for them, and re-layouts  1.25 us (1%)
    pallas_call x1, Pallas kernels, attention(): pl.pallas_call(attention_kernel, out_shape=out_shape, in_specs=[any_spec,...  50.4 us
    pallas_call x2, Pallas kernels, weight_gradient(): pl.pallas_call(functools.partial(weight_kernel, kv), in_specs=[any_spec]...  21.3 us
    ppermute x3, starting transfers between devices, fused_shards(): gm = gm + lax.ppermute(gm_parts[k], 'mp', ring)  4.71 us
    ppermute x3, starting transfers between devices, fused_shards(): lax.ppermute(gm, 'dp', [(i, (i + k) % DP) for i in range(DP)])  3.12 us
  transfers between devices with their start and end apart: 6, of which 0 were waited for; matrix products, arithmetic and copies ran while one was open for 0% of the time, Pallas kernels for 26%

profile of v5, /device:TPU:0, one launch (start us, length us, event | category | flops | bytes accessed | tf_op | source)
XLA Modules:
  0.0 83.2 jit_solution(6674789608944536846)
XLA Ops:
  0.6 50.4 %attention.1 = (bf16[3,512,512]{2,1,0:T(8,128)(2,1)}, bf16[3,512,512]{2,1,0:T(8,128)(2,1)}, bf16[3,2,512,128]{3,2,1,0:T(8,128)(2,1)}, bf16[4,2,4,16,1024]{4,3,2,...) custom-call(bf16[3,512,512]{2,1,0:T(8,128)(2,1)} %q_hbm.1, ...), custom_call_target="tpu_custom_call" | custom-call | flops 8000000000 | bytes 35000000 | tf_op jit(solution)/shard_map/attention/pallas_call | solution.py:379
  51.0 1.1 %collective-permute-start = (f32[16,1024]{1,0:T(8,128)}, f32[16,1024]{1,0:T(8,128)S(1)}, u32[]{:S(2)}, u32[]{:S(2)}) collective-permute-start(f32[16,1024]{1,0:T(8,128)} %get-tuple-element.27), channel_id=1, source_target_pairs={{0,2},{1,3},{2,4},{3,5},{4,6},{5,7},{6,0},{7,1},{8,10},{9,11},{10,... | collective-permute-start | bytes 196616 | tf_op jit(solution)/shard_map/ppermute | solution.py:544
  52.1 2.7 %collective-permute-start.1 = (f32[16,1024]{1,0:T(8,128)}, f32[16,1024]{1,0:T(8,128)S(1)}, u32[]{:S(2)}, u32[]{:S(2)}) collective-permute-start(f32[16,1024]{1,0:T(8,128)} %get-tuple-element.28), channel_id=1, source_target_pairs={{0,4},{1,5},{2,6},{3,7},{4,0},{5,1},{6,2},{7,3},{8,12},{9,13},{10,... | collective-permute-start | bytes 196616 | tf_op jit(solution)/shard_map/ppermute | solution.py:544
  54.8 0.9 %collective-permute-start.2 = (f32[16,1024]{1,0:T(8,128)}, f32[16,1024]{1,0:T(8,128)S(1)}, u32[]{:S(2)}, u32[]{:S(2)}) collective-permute-start(f32[16,1024]{1,0:T(8,128)} %get-tuple-element.29), channel_id=1, source_target_pairs={{0,6},{1,7},{2,0},{3,1},{4,2},{5,3},{6,4},{7,5},{8,14},{9,15},{10,... | collective-permute-start | bytes 196616 | tf_op jit(solution)/shard_map/ppermute | solution.py:544
  55.7 0.0 copy-start.1
  55.7 10.7 %grad_w_key.1 = (f32[3,512,4096]{2,1,0:T(8,128)}, bf16[3,512,512]{2,1,0:T(8,128)(2,1)}) custom-call(bf16[3,2,512,128]{3,2,1,0:T(8,128)(2,1)} %get-tuple-element.19.kvg_hbm, bf16[4,128,1024]{2,1,0:T(8,128)(2,1)} %bitcast.1, bf16[3,512,512]{2,1,0:T(8,128)(2,1)} %get-tuple-element.21.turned_hbm), custom_call_target="tpu_custom_call" | custom-call | flops 1610612736 | bytes 28311552 | tf_op jit(solution)/shard_map/grad_w_key/pallas_call | solution.py:494
  66.4 0.0 collective-permute-done
  66.4 0.0 collective-permute-done.1
  66.4 0.0 collective-permute-done.2
  66.5 0.0 copy-done.1
  66.5 0.0 copy-start
  66.5 1.5 %collective-permute-start.5 = (f32[16,1024]{1,0:T(8,128)S(1)}, f32[16,1024]{1,0:T(8,128)S(1)}, u32[]{:S(2)}, u32[]{:S(2)}) collective-permute-start(f32[16,1024]{1,0:T(8,128)S(1)} %add_add_fusion.refs_0_), channel_id=1, source_target_pairs={{0,24},{8,0},{16,8},{24,16},{1,25},{9,1},{17,9},{25,17},{2,26},{10... | collective-permute-start | bytes 196616 | tf_op jit(solution)/shard_map/ppermute | solution.py:548
  68.0 1.0 %collective-permute-start.4 = (f32[16,1024]{1,0:T(8,128)S(1)}, f32[16,1024]{1,0:T(8,128)S(1)}, u32[]{:S(2)}, u32[]{:S(2)}) collective-permute-start(f32[16,1024]{1,0:T(8,128)S(1)} %add_add_fusion.refs_0_), channel_id=1, source_target_pairs={{0,16},{8,24},{16,0},{24,8},{1,17},{9,25},{17,1},{25,9},{2,18},{10... | collective-permute-start | bytes 196616 | tf_op jit(solution)/shard_map/ppermute | solution.py:548
  69.1 0.6 collective-permute-start.3
  69.6 10.7 %grad_w_value.1 = (f32[3,512,4096]{2,1,0:T(8,128)}, bf16[3,512,512]{2,1,0:T(8,128)(2,1)}) custom-call(bf16[3,2,512,128]{3,2,1,0:T(8,128)(2,1)} %get-tuple-element.19.kvg_hbm, bf16[4,128,1024]{2,1,0:T(8,128)(2,1)} %bitcast.2, bf16[3,512,512]{2,1,0:T(8,128)(2,1)} %get-tuple-element.23.turned_hbm), custom_call_target="tpu_custom_call" | custom-call | flops 1610612736 | bytes 28311552 | tf_op jit(solution)/shard_map/grad_w_value/pallas_call | solution.py:494
  80.3 0.0 copy-done
  80.3 0.0 collective-permute-done.5.refs_3_
  80.3 0.0 copy-start.2
  80.3 0.0 collective-permute-done.4.refs_2_
  80.3 0.0 copy-start.3
  80.3 0.0 collective-permute-done.3.refs_1_
  80.3 0.6 copy-done.2
  80.9 0.0 copy-done.3
  81.0 0.0 copy-start.4
  81.0 0.6 copy-done.4
  81.6 1.7 %place.1 = f32[16,4096]{1,0:T(8,128)} custom-call(f32[16,1024]{1,0:T(8,128)} %copy-done, f32[16,1024]{1,0:T(8,128)} %copy-done.4, f32[16,1024]{1,0:T(8,128)} %copy-done.3, f32[16,1024]{1,0:T(8,128)} %copy-done.2), custom_call_target="tpu_custom_call" | custom-call | tf_op jit(solution)/shard_map/place/pallas_call | solution.py:551
  (1 shorter events, 0.0 us)
Async XLA Ops:
  51.0 15.4 %collective-permute-start = (f32[16,1024]{1,0:T(8,128)}, f32[16,1024]{1,0:T(8,128)S(1)}, u32[]{:S(2)}, u32[]{:S(2)}) collective-permute-start(f32[16,1024]{1,0:T(8,128)} %get-tuple-element.27), channel_id=1, source_target_pairs={{0,2},{1,3},{2,4},{3,5},{4,6},{5,7},{6,0},{7,1},{8,10},{9,11},{10,... | collective-permute-start | bytes 196616 | tf_op jit(solution)/shard_map/ppermute | solution.py:544
  52.1 14.3 %collective-permute-start.1 = (f32[16,1024]{1,0:T(8,128)}, f32[16,1024]{1,0:T(8,128)S(1)}, u32[]{:S(2)}, u32[]{:S(2)}) collective-permute-start(f32[16,1024]{1,0:T(8,128)} %get-tuple-element.28), channel_id=1, source_target_pairs={{0,4},{1,5},{2,6},{3,7},{4,0},{5,1},{6,2},{7,3},{8,12},{9,13},{10,... | collective-permute-start | bytes 196616 | tf_op jit(solution)/shard_map/ppermute | solution.py:544
  54.8 11.7 %collective-permute-start.2 = (f32[16,1024]{1,0:T(8,128)}, f32[16,1024]{1,0:T(8,128)S(1)}, u32[]{:S(2)}, u32[]{:S(2)}) collective-permute-start(f32[16,1024]{1,0:T(8,128)} %get-tuple-element.29), channel_id=1, source_target_pairs={{0,6},{1,7},{2,0},{3,1},{4,2},{5,3},{6,4},{7,5},{8,14},{9,15},{10,... | collective-permute-start | bytes 196616 | tf_op jit(solution)/shard_map/ppermute | solution.py:544
  55.7 10.7 %copy-start.1 = (f32[16,1024]{1,0:T(8,128)S(1)}, f32[16,1024]{1,0:T(8,128)}, u32[]{:S(2)}) copy-start(f32[16,1024]{1,0:T(8,128)} %get-tuple-element.26) | copy-start | bytes 196612
  66.5 13.8 %copy-start = (f32[16,1024]{1,0:T(8,128)}, f32[16,1024]{1,0:T(8,128)S(1)}, u32[]{:S(2)}) copy-start(f32[16,1024]{1,0:T(8,128)S(1)} %add_add_fusion.refs_0_) | copy-start | bytes 196612
  66.5 13.8 %collective-permute-start.5 = (f32[16,1024]{1,0:T(8,128)S(1)}, f32[16,1024]{1,0:T(8,128)S(1)}, u32[]{:S(2)}, u32[]{:S(2)}) collective-permute-start(f32[16,1024]{1,0:T(8,128)S(1)} %add_add_fusion.refs_0_), channel_id=1, source_target_pairs={{0,24},{8,0},{16,8},{24,16},{1,25},{9,1},{17,9},{25,17},{2,26},{10... | collective-permute-start | bytes 196616 | tf_op jit(solution)/shard_map/ppermute | solution.py:548
  68.0 12.3 %collective-permute-start.4 = (f32[16,1024]{1,0:T(8,128)S(1)}, f32[16,1024]{1,0:T(8,128)S(1)}, u32[]{:S(2)}, u32[]{:S(2)}) collective-permute-start(f32[16,1024]{1,0:T(8,128)S(1)} %add_add_fusion.refs_0_), channel_id=1, source_target_pairs={{0,16},{8,24},{16,0},{24,8},{1,17},{9,25},{17,1},{25,9},{2,18},{10... | collective-permute-start | bytes 196616 | tf_op jit(solution)/shard_map/ppermute | solution.py:548
  69.1 11.3 %collective-permute-start.3 = (f32[16,1024]{1,0:T(8,128)S(1)}, f32[16,1024]{1,0:T(8,128)S(1)}, u32[]{:S(2)}, u32[]{:S(2)}) collective-permute-start(f32[16,1024]{1,0:T(8,128)S(1)} %add_add_fusion.refs_0_), channel_id=1, source_target_pairs={{0,8},{8,16},{16,24},{24,0},{1,9},{9,17},{17,25},{25,1},{2,10},{10... | collective-permute-start | bytes 196616 | tf_op jit(solution)/shard_map/ppermute | solution.py:548
  80.3 0.6 copy-start.2
  80.3 0.6 copy-start.3
  81.0 0.6 copy-start.4

commit v6 on v5

--- a/solution.py
+++ b/solution.py
@@ -40,7 +40,7 @@
     x, y = i % 2, i // 2
     i_x, i_y, i_far = y * 2 + 1 - x, (1 - y) * 2 + x, DP - 1 - i
     order = (i, i_x, i_y, i_far)
-    to_x, to_y = {"dp": i_x, "mp": me}, {"dp": i_y, "mp": me}
+    to_x, to_y, to_far = ({"dp": j, "mp": me} for j in (i_x, i_y, i_far))
 
     sib = {"dp": i, "mp": sibling}
 
@@ -69,10 +69,10 @@
     barrier = pltpu.get_barrier_semaphore()
     for k in range(1, CHIPS):
         pl.semaphore_signal(barrier, inc=1, device_id=z_peer(k), device_id_type=MESH)
-    for peer in (to_x, to_y, sib):
+    for peer in (to_x, to_y, to_far, sib):
         pl.semaphore_signal(barrier, inc=1, device_id=peer, device_id_type=MESH)
     load_mem.wait()
-    pl.semaphore_wait(barrier, CHIPS - 1 + 3)
+    pl.semaphore_wait(barrier, CHIPS - 1 + 4)
 
     mine = columns(0)
     z_copies = []
@@ -202,18 +202,13 @@
         return landed[layer, slot].astype(F32)
 
     def ag_copy(layer, at):
-        block = (
-            kvg.at[layer, :, pair_rows(i), :],
-            kvg.at[layer, :, pair_rows(i), :],
-            kvg.at[layer, 0, pair_rows(i_x), :],
-            kvg.at[layer, 1, pair_rows(i_y), :],
-        )[at]
+        block = kvg.at[layer, :, pair_rows(i), :]
         return pltpu.make_async_remote_copy(
             src_ref=block,
             dst_ref=block,
             send_sem=ag_send.at[layer, at],
             recv_sem=ag_recv.at[layer, at],
-            device_id=(to_x, to_y, to_y, to_x)[at],
+            device_id=(to_far, to_x, to_y)[at],
             device_id_type=MESH,
         )
 
@@ -222,13 +217,8 @@
         values = own[layer, 1] + came(layer, 3) + came(layer, 4)
         kvg[layer, 0, pair_rows(i), :] = keys.astype(BF16)
         kvg[layer, 1, pair_rows(i), :] = values.astype(BF16)
-        ag_copy(layer, 0).start()
-        ag_copy(layer, 1).start()
-
-    def pass_on(layer):
-        for near in range(2):
-            ag_copy(layer, near).wait_recv()
-            ag_copy(layer, 2 + near).start()
+        for at in range(DP - 1):
+            ag_copy(layer, at).start()
 
     def head_masks(axis):
         return lax.broadcasted_iota(jnp.int32, (PAIR, PAIR), axis) < HEAD_WIDTH
@@ -304,12 +294,8 @@
         send_part(layer, 4, hold[0] + came(layer, 1))
         send_part(layer, 5, hold[1] + came(layer, 0))
 
-        @pl.when(layer >= 1)
-        def _():
-            pass_on(layer - 1)
-
     def add_memory_gradient(layer):
-        for at in (2, 3):
+        for at in range(DP - 1):
             ag_copy(layer, at).wait_recv()
         for kv in range(2):
             term = lax.dot_general(
@@ -330,8 +316,6 @@
     att_out.start()
     gq_out.start()
     for layer in range(layers):
-        if layer == layers - 1:
-            pass_on(layer)
         add_memory_gradient(layer)
     kvg_out = pltpu.make_async_copy(kvg, kvg_hbm, out_sem.at[3])
     kvg_out.start()
@@ -349,7 +333,7 @@
     for layer in range(layers):
         for slot in range(6):
             rs_copy(layer, slot).wait_send()
-        for at in range(4):
+        for at in range(DP - 1):
             ag_copy(layer, at).wait_send()
     gm_copy.wait()
     gm_landed[...] += gm_v[core]
@@ -412,8 +396,8 @@
             dma((DP,)),
             dma((layers, 6)),
             dma((layers, 6)),
-            dma((layers, 4)),
-            dma((layers, 4)),
+            dma((layers, DP - 1)),
+            dma((layers, DP - 1)),
             dma((2,)),
         ],
         compiler_params=pltpu.CompilerParams(
@@ -443,19 +427,25 @@
     loads[0].wait()
     loads[1].wait()
 
+    rows = ring.shape[1]
+    blocks = width // rows
+
+    def block_rows(n):
+        return pl.ds(pl.multiple_of(n % blocks * rows, rows), rows)
+
     def write(n):
-        at = pl.ds(pl.multiple_of(n % DP * PAIR, PAIR), PAIR)
         return pltpu.make_async_copy(
-            ring.at[n % slots], out_hbm.at[n // DP, at, :], ring_sem.at[n % slots]
+            ring.at[n % slots],
+            out_hbm.at[n // blocks, block_rows(n), :],
+            ring_sem.at[n % slots],
         )
 
     def write_back(layer):
         return pltpu.make_async_copy(back_v.at[layer], back_hbm.at[layer], back_sem.at[layer])
 
-    @pl.loop(0, layers * DP)
+    @pl.loop(0, layers * blocks)
     def step(n):
-        layer = n // DP
-        at = pl.ds(pl.multiple_of(n % DP * PAIR, PAIR), PAIR)
+        layer = n // blocks
 
         @pl.when(n >= slots)
         def _():
@@ -463,7 +453,7 @@
 
         for j in range(DP):
             ring[n % slots, :, j * quarter : (j + 1) * quarter] = jnp.dot(
-                kvg_v[layer, at, :], mem_v[j], preferred_element_type=F32
+                kvg_v[layer, block_rows(n), :], mem_v[j], preferred_element_type=F32
             )
         write(n).start()
 
@@ -471,13 +461,13 @@
         def _():
             loads[2].wait()
 
-        back_v[layer, :, at] = turned_v[layer, at, :].T
-
-        @pl.when(n % DP == DP - 1)
+        back_v[layer, :, block_rows(n)] = turned_v[layer, block_rows(n), :].T
+
+        @pl.when(n % blocks == blocks - 1)
         def _():
             write_back(layer).start()
 
-    for n in range(layers * DP - slots, layers * DP):
+    for n in range(layers * blocks - slots, layers * blocks):
         write(n).wait()
     for layer in range(layers):
         write_back(layer).wait()
@@ -503,7 +493,7 @@
             pltpu.VMEM((layers, width, mem_total), BF16),
             pltpu.VMEM(mem.shape, BF16),
             pltpu.VMEM(turned.shape, BF16),
-            pltpu.VMEM((slots, PAIR, model), F32),
+            pltpu.VMEM((slots, 2 * PAIR, model), F32),
             pltpu.VMEM((layers, rows, width), BF16),
             dma((3,)),
             dma((slots,)),
@@ -520,12 +510,17 @@
 
 
 def place_kernel(*refs):
-    out_ref = refs[-1]
+    out_ref, sem = refs[-2:]
     quarter = refs[0].shape[-1]
     i = lax.axis_index("dp")
-    for k, ref in enumerate(refs[:-1]):
+    copies = []
+    for k, ref in enumerate(refs[:-2]):
         j = (i + DP - k) % DP
-        out_ref[:, pl.ds(pl.multiple_of(j * quarter, quarter), quarter)] = ref[...]
+        cols = pl.ds(pl.multiple_of(j * quarter, quarter), quarter)
+        copies.append(pltpu.make_async_copy(ref, out_ref.at[:, cols], sem.at[k]))
+        copies[-1].start()
+    for copy in copies:
+        copy.wait()
 
 
 def fused_shards(queries, memory, w_key, w_value, grad_out):
@@ -550,9 +545,10 @@
     grad_w_value, grad_queries = weight_gradient(kvg, mem, grad_queries_t, 1)
     grad_memory = pl.pallas_call(
         place_kernel,
-        in_specs=[pl.BlockSpec(memory_space=pltpu.VMEM)] * DP,
-        out_specs=pl.BlockSpec(memory_space=pltpu.VMEM),
+        in_specs=[pl.BlockSpec(memory_space=pl.ANY)] * DP,
+        out_specs=pl.BlockSpec(memory_space=pl.ANY),
         out_shape=jax.ShapeDtypeStruct((tokens, model), F32),
+        scratch_shapes=[pltpu.SemaphoreType.DMA((DP,))],
         name="place",
     )(*quarters)
     return attended, grad_queries, grad_memory, grad_w_key, grad_w_value

time: 83.5 us -> 91.3 us (1.093)
  Pallas kernels: 73.4 us -> 80.5 us
    pallas_call x1, Pallas kernels: 1.67 us -> 9.08 us  [fused_shards(): pl.pallas_call(place_kernel, in_specs=[pl.BlockSpec(memory_space=pl.ANY)]...]
  transfers between devices with their start and end apart: 6 -> 6, of which waited for: 0 -> 0; matrix products, arithmetic and copies ran while one was open for 0% -> 0% of each run, Pallas kernels for 26% -> 24%
where the time goes in v6:
time: 91.3 us; the launch traced here: 91.1 us
  Pallas kernels  80.5 us (88%)
  starting transfers between devices  8.61 us (9%)
  local copies, waits for them, and re-layouts  1.25 us (1%)
    pallas_call x1, Pallas kernels, attention(): pl.pallas_call(attention_kernel, out_shape=out_shape, in_specs=[any_spec,...  49.5 us
    pallas_call x2, Pallas kernels, weight_gradient(): pl.pallas_call(functools.partial(weight_kernel, kv), in_specs=[any_spec]...  21.9 us
    pallas_call x1, Pallas kernels, fused_shards(): pl.pallas_call(place_kernel, in_specs=[pl.BlockSpec(memory_space=pl.ANY)]...  9.08 us
    ppermute x3, starting transfers between devices, fused_shards(): gm = gm + lax.ppermute(gm_parts[k], 'mp', ring)  5.42 us
    ppermute x3, starting transfers between devices, fused_shards(): lax.ppermute(gm, 'dp', [(i, (i + k) % DP) for i in range(DP)])  3.19 us
  transfers between devices with their start and end apart: 6, of which 0 were waited for; matrix products, arithmetic and copies ran while one was open for 0% of the time, Pallas kernels for 24%

profile of v6, /device:TPU:0, one launch (start us, length us, event | category | flops | bytes accessed | tf_op | source)
XLA Modules:
  0.0 91.1 jit_solution(7618694835342246150)
XLA Ops:
  0.6 49.5 %attention.1 = (bf16[3,512,512]{2,1,0:T(8,128)(2,1)}, bf16[3,512,512]{2,1,0:T(8,128)(2,1)}, bf16[3,2,512,128]{3,2,1,0:T(8,128)(2,1)}, bf16[4,2,4,16,1024]{4,3,2,...) custom-call(bf16[3,512,512]{2,1,0:T(8,128)(2,1)} %q_hbm.1, ...), custom_call_target="tpu_custom_call" | custom-call | flops 8000000000 | bytes 35000000 | tf_op jit(solution)/shard_map/attention/pallas_call | solution.py:363
  50.2 1.9 %collective-permute-start = (f32[16,1024]{1,0:T(8,128)}, f32[16,1024]{1,0:T(8,128)S(1)}, u32[]{:S(2)}, u32[]{:S(2)}) collective-permute-start(f32[16,1024]{1,0:T(8,128)} %get-tuple-element.27), channel_id=1, source_target_pairs={{0,2},{1,3},{2,4},{3,5},{4,6},{5,7},{6,0},{7,1},{8,10},{9,11},{10,... | collective-permute-start | bytes 196616 | tf_op jit(solution)/shard_map/ppermute | solution.py:539
  52.1 2.6 %collective-permute-start.1 = (f32[16,1024]{1,0:T(8,128)}, f32[16,1024]{1,0:T(8,128)S(1)}, u32[]{:S(2)}, u32[]{:S(2)}) collective-permute-start(f32[16,1024]{1,0:T(8,128)} %get-tuple-element.28), channel_id=1, source_target_pairs={{0,4},{1,5},{2,6},{3,7},{4,0},{5,1},{6,2},{7,3},{8,12},{9,13},{10,... | collective-permute-start | bytes 196616 | tf_op jit(solution)/shard_map/ppermute | solution.py:539
  54.7 0.9 %collective-permute-start.2 = (f32[16,1024]{1,0:T(8,128)}, f32[16,1024]{1,0:T(8,128)S(1)}, u32[]{:S(2)}, u32[]{:S(2)}) collective-permute-start(f32[16,1024]{1,0:T(8,128)} %get-tuple-element.29), channel_id=1, source_target_pairs={{0,6},{1,7},{2,0},{3,1},{4,2},{5,3},{6,4},{7,5},{8,14},{9,15},{10,... | collective-permute-start | bytes 196616 | tf_op jit(solution)/shard_map/ppermute | solution.py:539
  55.6 0.0 copy-start.1
  55.6 10.9 %grad_w_key.1 = (f32[3,512,4096]{2,1,0:T(8,128)}, bf16[3,512,512]{2,1,0:T(8,128)(2,1)}) custom-call(bf16[3,2,512,128]{3,2,1,0:T(8,128)(2,1)} %get-tuple-element.19.kvg_hbm, bf16[4,128,1024]{2,1,0:T(8,128)(2,1)} %bitcast.1, bf16[3,512,512]{2,1,0:T(8,128)(2,1)} %get-tuple-element.21.turned_hbm), custom_call_target="tpu_custom_call" | custom-call | flops 1610612736 | bytes 28311552 | tf_op jit(solution)/shard_map/grad_w_key/pallas_call | solution.py:484
  66.6 0.0 collective-permute-done
  66.6 0.0 collective-permute-done.1
  66.6 0.0 collective-permute-done.2
  66.6 0.0 copy-done.1
  66.6 0.0 copy-start
  66.6 1.5 %collective-permute-start.5 = (f32[16,1024]{1,0:T(8,128)S(1)}, f32[16,1024]{1,0:T(8,128)S(1)}, u32[]{:S(2)}, u32[]{:S(2)}) collective-permute-start(f32[16,1024]{1,0:T(8,128)S(1)} %add_add_fusion.refs_0_), channel_id=1, source_target_pairs={{0,24},{8,0},{16,8},{24,16},{1,25},{9,1},{17,9},{25,17},{2,26},{10... | collective-permute-start | bytes 196616 | tf_op jit(solution)/shard_map/ppermute | solution.py:543
  68.2 1.1 %collective-permute-start.4 = (f32[16,1024]{1,0:T(8,128)S(1)}, f32[16,1024]{1,0:T(8,128)S(1)}, u32[]{:S(2)}, u32[]{:S(2)}) collective-permute-start(f32[16,1024]{1,0:T(8,128)S(1)} %add_add_fusion.refs_0_), channel_id=1, source_target_pairs={{0,16},{8,24},{16,0},{24,8},{1,17},{9,25},{17,1},{25,9},{2,18},{10... | collective-permute-start | bytes 196616 | tf_op jit(solution)/shard_map/ppermute | solution.py:543
  69.3 0.6 collective-permute-start.3
  69.8 10.9 %grad_w_value.1 = (f32[3,512,4096]{2,1,0:T(8,128)}, bf16[3,512,512]{2,1,0:T(8,128)(2,1)}) custom-call(bf16[3,2,512,128]{3,2,1,0:T(8,128)(2,1)} %get-tuple-element.19.kvg_hbm, bf16[4,128,1024]{2,1,0:T(8,128)(2,1)} %bitcast.2, bf16[3,512,512]{2,1,0:T(8,128)(2,1)} %get-tuple-element.23.turned_hbm), custom_call_target="tpu_custom_call" | custom-call | flops 1610612736 | bytes 28311552 | tf_op jit(solution)/shard_map/grad_w_value/pallas_call | solution.py:484
  80.8 0.0 copy-done
  80.8 0.0 collective-permute-done.5.refs_3_
  80.8 0.0 copy-start.2
  80.8 0.0 collective-permute-done.4.refs_2_
  80.8 0.0 copy-start.3
  80.8 0.0 collective-permute-done.3.refs_1_
  80.8 0.6 copy-done.2
  81.4 0.0 copy-done.3
  81.4 0.0 copy-start.4
  81.4 0.6 copy-done.4
  82.1 9.1 %place.1 = f32[16,4096]{1,0:T(8,128)} custom-call(f32[16,1024]{1,0:T(8,128)} %copy-done, f32[16,1024]{1,0:T(8,128)} %copy-done.4, f32[16,1024]{1,0:T(8,128)} %copy-done.3, f32[16,1024]{1,0:T(8,128)} %copy-done.2), custom_call_target="tpu_custom_call" | custom-call | tf_op jit(solution)/shard_map/place/pallas_call | solution.py:546
  (1 shorter events, 0.0 us)
Async XLA Ops:
  50.2 16.4 %collective-permute-start = (f32[16,1024]{1,0:T(8,128)}, f32[16,1024]{1,0:T(8,128)S(1)}, u32[]{:S(2)}, u32[]{:S(2)}) collective-permute-start(f32[16,1024]{1,0:T(8,128)} %get-tuple-element.27), channel_id=1, source_target_pairs={{0,2},{1,3},{2,4},{3,5},{4,6},{5,7},{6,0},{7,1},{8,10},{9,11},{10,... | collective-permute-start | bytes 196616 | tf_op jit(solution)/shard_map/ppermute | solution.py:539
  52.1 14.5 %collective-permute-start.1 = (f32[16,1024]{1,0:T(8,128)}, f32[16,1024]{1,0:T(8,128)S(1)}, u32[]{:S(2)}, u32[]{:S(2)}) collective-permute-start(f32[16,1024]{1,0:T(8,128)} %get-tuple-element.28), channel_id=1, source_target_pairs={{0,4},{1,5},{2,6},{3,7},{4,0},{5,1},{6,2},{7,3},{8,12},{9,13},{10,... | collective-permute-start | bytes 196616 | tf_op jit(solution)/shard_map/ppermute | solution.py:539
  54.7 11.9 %collective-permute-start.2 = (f32[16,1024]{1,0:T(8,128)}, f32[16,1024]{1,0:T(8,128)S(1)}, u32[]{:S(2)}, u32[]{:S(2)}) collective-permute-start(f32[16,1024]{1,0:T(8,128)} %get-tuple-element.29), channel_id=1, source_target_pairs={{0,6},{1,7},{2,0},{3,1},{4,2},{5,3},{6,4},{7,5},{8,14},{9,15},{10,... | collective-permute-start | bytes 196616 | tf_op jit(solution)/shard_map/ppermute | solution.py:539
  55.6 11.0 %copy-start.1 = (f32[16,1024]{1,0:T(8,128)S(1)}, f32[16,1024]{1,0:T(8,128)}, u32[]{:S(2)}) copy-start(f32[16,1024]{1,0:T(8,128)} %get-tuple-element.26) | copy-start | bytes 196612
  66.6 14.1 %copy-start = (f32[16,1024]{1,0:T(8,128)}, f32[16,1024]{1,0:T(8,128)S(1)}, u32[]{:S(2)}) copy-start(f32[16,1024]{1,0:T(8,128)S(1)} %add_add_fusion.refs_0_) | copy-start | bytes 196612
  66.6 14.1 %collective-permute-start.5 = (f32[16,1024]{1,0:T(8,128)S(1)}, f32[16,1024]{1,0:T(8,128)S(1)}, u32[]{:S(2)}, u32[]{:S(2)}) collective-permute-start(f32[16,1024]{1,0:T(8,128)S(1)} %add_add_fusion.refs_0_), channel_id=1, source_target_pairs={{0,24},{8,0},{16,8},{24,16},{1,25},{9,1},{17,9},{25,17},{2,26},{10... | collective-permute-start | bytes 196616 | tf_op jit(solution)/shard_map/ppermute | solution.py:543
  68.2 12.6 %collective-permute-start.4 = (f32[16,1024]{1,0:T(8,128)S(1)}, f32[16,1024]{1,0:T(8,128)S(1)}, u32[]{:S(2)}, u32[]{:S(2)}) collective-permute-start(f32[16,1024]{1,0:T(8,128)S(1)} %add_add_fusion.refs_0_), channel_id=1, source_target_pairs={{0,16},{8,24},{16,0},{24,8},{1,17},{9,25},{17,1},{25,9},{2,18},{10... | collective-permute-start | bytes 196616 | tf_op jit(solution)/shard_map/ppermute | solution.py:543
  69.3 11.6 %collective-permute-start.3 = (f32[16,1024]{1,0:T(8,128)S(1)}, f32[16,1024]{1,0:T(8,128)S(1)}, u32[]{:S(2)}, u32[]{:S(2)}) collective-permute-start(f32[16,1024]{1,0:T(8,128)S(1)} %add_add_fusion.refs_0_), channel_id=1, source_target_pairs={{0,8},{8,16},{16,24},{24,0},{1,9},{9,17},{17,25},{25,1},{2,10},{10... | collective-permute-start | bytes 196616 | tf_op jit(solution)/shard_map/ppermute | solution.py:543
  80.8 0.6 copy-start.2
  80.8 0.6 copy-start.3
  81.4 0.6 copy-start.4

commit v7 on v6

--- a/solution.py
+++ b/solution.py
@@ -47,12 +47,9 @@
     def columns(step):
         return pl.ds(pl.multiple_of(order[step] * quarter, quarter), quarter)
 
-    def load_w(step):
-        cols = columns(step)
+    def load_w(layer):
         return [
-            pltpu.make_async_copy(
-                hbm.at[:, :, cols], w_v.at[:, kv, :, cols], w_sem.at[step, kv]
-            )
+            pltpu.make_async_copy(hbm.at[layer], w_v.at[layer, kv], w_sem.at[layer, kv])
             for kv, hbm in enumerate((wk_hbm, wv_hbm))
         ]
 
@@ -62,8 +59,8 @@
     load_mem.start()
     load_q.start()
     load_g.start()
-    for step in range(DP):
-        for copy in load_w(step):
+    for layer in range(layers):
+        for copy in load_w(layer):
             copy.start()
 
     barrier = pltpu.get_barrier_semaphore()
@@ -76,10 +73,11 @@
 
     mine = columns(0)
     z_copies = []
+    mg[i, core, z] = mem_ref[:, mine]
     for k in range(1, CHIPS):
         z_copies.append(
             pltpu.make_async_remote_copy(
-                src_ref=mem_ref.at[:, mine],
+                src_ref=mg.at[i, core, z],
                 dst_ref=mg.at[i, core, z],
                 send_sem=z_send.at[k - 1],
                 recv_sem=z_recv.at[k - 1],
@@ -88,7 +86,6 @@
             )
         )
         z_copies[-1].start()
-    mg[i, core, z] = mem_ref[:, mine]
     for copy in z_copies:
         copy.wait_recv()
 
@@ -150,15 +147,17 @@
             d_copies[2].wait_recv()
             d_copies[3].wait_recv()
             s_copies[3].start()
-        for copy in load_w(step):
-            copy.wait()
         s_copies[step].wait_recv()
         mt[step] = mg[order[step]].reshape(mem_total, quarter).T
         if step == 0:
 
-            @pl.loop(0, layers * 2)
-            def first_quarter(n):
-                acc[n // 2, n % 2] = project(n // 2, n % 2, 0)
+            for layer in range(layers):
+                for copy in load_w(layer):
+                    copy.wait()
+
+                @pl.loop(0, 2)
+                def first_quarter(kv):
+                    acc[layer, kv] = project(layer, kv, 0)
 
         elif step < DP - 1:
 
@@ -386,7 +385,7 @@
             pltpu.VMEM((CORES, CHIPS, tokens, quarter), F32),
             pltpu.VMEM((CHIPS, tokens, quarter), F32),
             dma((3,)),
-            dma((DP, 2)),
+            dma((layers, 2)),
             dma((4 + CHIPS,)),
             dma((CHIPS - 1,)),
             dma((CHIPS - 1,)),
@@ -493,7 +492,7 @@
             pltpu.VMEM((layers, width, mem_total), BF16),
             pltpu.VMEM(mem.shape, BF16),
             pltpu.VMEM(turned.shape, BF16),
-            pltpu.VMEM((slots, 2 * PAIR, model), F32),
+            pltpu.VMEM((slots, PAIR, model), F32),
             pltpu.VMEM((layers, rows, width), BF16),
             dma((3,)),
             dma((slots,)),
@@ -510,17 +509,12 @@
 
 
 def place_kernel(*refs):
-    out_ref, sem = refs[-2:]
+    out_ref = refs[-1]
     quarter = refs[0].shape[-1]
     i = lax.axis_index("dp")
-    copies = []
-    for k, ref in enumerate(refs[:-2]):
+    for k, ref in enumerate(refs[:-1]):
         j = (i + DP - k) % DP
-        cols = pl.ds(pl.multiple_of(j * quarter, quarter), quarter)
-        copies.append(pltpu.make_async_copy(ref, out_ref.at[:, cols], sem.at[k]))
-        copies[-1].start()
-    for copy in copies:
-        copy.wait()
+        out_ref[:, pl.ds(pl.multiple_of(j * quarter, quarter), quarter)] = ref[...]
 
 
 def fused_shards(queries, memory, w_key, w_value, grad_out):
@@ -545,10 +539,9 @@
     grad_w_value, grad_queries = weight_gradient(kvg, mem, grad_queries_t, 1)
     grad_memory = pl.pallas_call(
         place_kernel,
-        in_specs=[pl.BlockSpec(memory_space=pl.ANY)] * DP,
-        out_specs=pl.BlockSpec(memory_space=pl.ANY),
+        in_specs=[pl.BlockSpec(memory_space=pltpu.VMEM)] * DP,
+        out_specs=pl.BlockSpec(memory_space=pltpu.VMEM),
         out_shape=jax.ShapeDtypeStruct((tokens, model), F32),
-        scratch_shapes=[pltpu.SemaphoreType.DMA((DP,))],
         name="place",
     )(*quarters)
     return attended, grad_queries, grad_memory, grad_w_key, grad_w_value

time: 91.3 us -> 86.1 us (0.943)
  Pallas kernels: 80.5 us -> 76.4 us
  starting transfers between devices: 8.61 us -> 7.43 us
    pallas_call x1, Pallas kernels: 9.08 us -> 1.67 us  [fused_shards(): pl.pallas_call(place_kernel, in_specs=[pl.BlockSpec(memory_space=pltpu.VM...]
    pallas_call x1, Pallas kernels: 49.5 us -> 53.4 us  [attention(): pl.pallas_call(attention_kernel, out_shape=out_shape, in_specs=[any_spec,...]
    ppermute x3, starting transfers between devices: 5.42 us -> 4.24 us  [fused_shards(): gm = gm + lax.ppermute(gm_parts[k], 'mp', ring)]
  transfers between devices with their start and end apart: 6 -> 6, of which waited for: 0 -> 0; matrix products, arithmetic and copies ran while one was open for 0% -> 0% of each run, Pallas kernels for 24% -> 25%
where the time goes in v7:
time: 86.1 us; the launch traced here: 85.8 us
  Pallas kernels  76.4 us (89%)
  starting transfers between devices  7.43 us (9%)
  local copies, waits for them, and re-layouts  1.25 us (1%)
    pallas_call x1, Pallas kernels, attention(): pl.pallas_call(attention_kernel, out_shape=out_shape, in_specs=[any_spec,...  53.4 us
    pallas_call x2, Pallas kernels, weight_gradient(): pl.pallas_call(functools.partial(weight_kernel, kv), in_specs=[any_spec]...  21.3 us
    ppermute x3, starting transfers between devices, fused_shards(): gm = gm + lax.ppermute(gm_parts[k], 'mp', ring)  4.24 us
    ppermute x3, starting transfers between devices, fused_shards(): lax.ppermute(gm, 'dp', [(i, (i + k) % DP) for i in range(DP)])  3.19 us
  transfers between devices with their start and end apart: 6, of which 0 were waited for; matrix products, arithmetic and copies ran while one was open for 0% of the time, Pallas kernels for 25%

profile of v7, /device:TPU:0, one launch (start us, length us, event | category | flops | bytes accessed | tf_op | source)
XLA Modules:
  0.0 85.8 jit_solution(4543616233726819476)
XLA Ops:
  0.6 53.4 %attention.1 = (bf16[3,512,512]{2,1,0:T(8,128)(2,1)}, bf16[3,512,512]{2,1,0:T(8,128)(2,1)}, bf16[3,2,512,128]{3,2,1,0:T(8,128)(2,1)}, bf16[4,2,4,16,1024]{4,3,2,...) custom-call(bf16[3,512,512]{2,1,0:T(8,128)(2,1)} %q_hbm.1, ...), custom_call_target="tpu_custom_call" | custom-call | flops 8000000000 | bytes 35000000 | tf_op jit(solution)/shard_map/attention/pallas_call | solution.py:362
  54.0 1.1 %collective-permute-start = (f32[16,1024]{1,0:T(8,128)}, f32[16,1024]{1,0:T(8,128)S(1)}, u32[]{:S(2)}, u32[]{:S(2)}) collective-permute-start(f32[16,1024]{1,0:T(8,128)} %get-tuple-element.27), channel_id=1, source_target_pairs={{0,2},{1,3},{2,4},{3,5},{4,6},{5,7},{6,0},{7,1},{8,10},{9,11},{10,... | collective-permute-start | bytes 196616 | tf_op jit(solution)/shard_map/ppermute | solution.py:533
  55.2 1.2 %collective-permute-start.1 = (f32[16,1024]{1,0:T(8,128)}, f32[16,1024]{1,0:T(8,128)S(1)}, u32[]{:S(2)}, u32[]{:S(2)}) collective-permute-start(f32[16,1024]{1,0:T(8,128)} %get-tuple-element.28), channel_id=1, source_target_pairs={{0,4},{1,5},{2,6},{3,7},{4,0},{5,1},{6,2},{7,3},{8,12},{9,13},{10,... | collective-permute-start | bytes 196616 | tf_op jit(solution)/shard_map/ppermute | solution.py:533
  56.4 1.9 %collective-permute-start.2 = (f32[16,1024]{1,0:T(8,128)}, f32[16,1024]{1,0:T(8,128)S(1)}, u32[]{:S(2)}, u32[]{:S(2)}) collective-permute-start(f32[16,1024]{1,0:T(8,128)} %get-tuple-element.29), channel_id=1, source_target_pairs={{0,6},{1,7},{2,0},{3,1},{4,2},{5,3},{6,4},{7,5},{8,14},{9,15},{10,... | collective-permute-start | bytes 196616 | tf_op jit(solution)/shard_map/ppermute | solution.py:533
  58.3 0.0 copy-start.1
  58.3 10.7 %grad_w_key.1 = (f32[3,512,4096]{2,1,0:T(8,128)}, bf16[3,512,512]{2,1,0:T(8,128)(2,1)}) custom-call(bf16[3,2,512,128]{3,2,1,0:T(8,128)(2,1)} %get-tuple-element.19.kvg_hbm, bf16[4,128,1024]{2,1,0:T(8,128)(2,1)} %bitcast.1, bf16[3,512,512]{2,1,0:T(8,128)(2,1)} %get-tuple-element.21.turned_hbm), custom_call_target="tpu_custom_call" | custom-call | flops 1610612736 | bytes 28311552 | tf_op jit(solution)/shard_map/grad_w_key/pallas_call | solution.py:483
  68.9 0.0 collective-permute-done
  69.0 0.0 collective-permute-done.1
  69.0 0.0 collective-permute-done.2
  69.0 0.0 copy-done.1
  69.0 0.0 copy-start
  69.0 1.5 %collective-permute-start.5 = (f32[16,1024]{1,0:T(8,128)S(1)}, f32[16,1024]{1,0:T(8,128)S(1)}, u32[]{:S(2)}, u32[]{:S(2)}) collective-permute-start(f32[16,1024]{1,0:T(8,128)S(1)} %add_add_fusion.refs_0_), channel_id=1, source_target_pairs={{0,24},{8,0},{16,8},{24,16},{1,25},{9,1},{17,9},{25,17},{2,26},{10... | collective-permute-start | bytes 196616 | tf_op jit(solution)/shard_map/ppermute | solution.py:537
  70.5 1.1 %collective-permute-start.4 = (f32[16,1024]{1,0:T(8,128)S(1)}, f32[16,1024]{1,0:T(8,128)S(1)}, u32[]{:S(2)}, u32[]{:S(2)}) collective-permute-start(f32[16,1024]{1,0:T(8,128)S(1)} %add_add_fusion.refs_0_), channel_id=1, source_target_pairs={{0,16},{8,24},{16,0},{24,8},{1,17},{9,25},{17,1},{25,9},{2,18},{10... | collective-permute-start | bytes 196616 | tf_op jit(solution)/shard_map/ppermute | solution.py:537
  71.6 0.6 collective-permute-start.3
  72.2 10.6 %grad_w_value.1 = (f32[3,512,4096]{2,1,0:T(8,128)}, bf16[3,512,512]{2,1,0:T(8,128)(2,1)}) custom-call(bf16[3,2,512,128]{3,2,1,0:T(8,128)(2,1)} %get-tuple-element.19.kvg_hbm, bf16[4,128,1024]{2,1,0:T(8,128)(2,1)} %bitcast.2, bf16[3,512,512]{2,1,0:T(8,128)(2,1)} %get-tuple-element.23.turned_hbm), custom_call_target="tpu_custom_call" | custom-call | flops 1610612736 | bytes 28311552 | tf_op jit(solution)/shard_map/grad_w_value/pallas_call | solution.py:483
  82.9 0.0 copy-done
  82.9 0.0 collective-permute-done.5.refs_3_
  82.9 0.0 copy-start.2
  82.9 0.0 collective-permute-done.4.refs_2_
  82.9 0.0 copy-start.3
  82.9 0.0 collective-permute-done.3.refs_1_
  82.9 0.6 copy-done.2
  83.5 0.0 copy-done.3
  83.6 0.0 copy-start.4
  83.6 0.6 copy-done.4
  84.2 1.7 %place.1 = f32[16,4096]{1,0:T(8,128)} custom-call(f32[16,1024]{1,0:T(8,128)} %copy-done, f32[16,1024]{1,0:T(8,128)} %copy-done.4, f32[16,1024]{1,0:T(8,128)} %copy-done.3, f32[16,1024]{1,0:T(8,128)} %copy-done.2), custom_call_target="tpu_custom_call" | custom-call | tf_op jit(solution)/shard_map/place/pallas_call | solution.py:540
  (1 shorter events, 0.0 us)
Async XLA Ops:
  54.0 14.9 %collective-permute-start = (f32[16,1024]{1,0:T(8,128)}, f32[16,1024]{1,0:T(8,128)S(1)}, u32[]{:S(2)}, u32[]{:S(2)}) collective-permute-start(f32[16,1024]{1,0:T(8,128)} %get-tuple-element.27), channel_id=1, source_target_pairs={{0,2},{1,3},{2,4},{3,5},{4,6},{5,7},{6,0},{7,1},{8,10},{9,11},{10,... | collective-permute-start | bytes 196616 | tf_op jit(solution)/shard_map/ppermute | solution.py:533
  55.2 13.8 %collective-permute-start.1 = (f32[16,1024]{1,0:T(8,128)}, f32[16,1024]{1,0:T(8,128)S(1)}, u32[]{:S(2)}, u32[]{:S(2)}) collective-permute-start(f32[16,1024]{1,0:T(8,128)} %get-tuple-element.28), channel_id=1, source_target_pairs={{0,4},{1,5},{2,6},{3,7},{4,0},{5,1},{6,2},{7,3},{8,12},{9,13},{10,... | collective-permute-start | bytes 196616 | tf_op jit(solution)/shard_map/ppermute | solution.py:533
  56.4 12.6 %collective-permute-start.2 = (f32[16,1024]{1,0:T(8,128)}, f32[16,1024]{1,0:T(8,128)S(1)}, u32[]{:S(2)}, u32[]{:S(2)}) collective-permute-start(f32[16,1024]{1,0:T(8,128)} %get-tuple-element.29), channel_id=1, source_target_pairs={{0,6},{1,7},{2,0},{3,1},{4,2},{5,3},{6,4},{7,5},{8,14},{9,15},{10,... | collective-permute-start | bytes 196616 | tf_op jit(solution)/shard_map/ppermute | solution.py:533
  58.3 10.7 %copy-start.1 = (f32[16,1024]{1,0:T(8,128)S(1)}, f32[16,1024]{1,0:T(8,128)}, u32[]{:S(2)}) copy-start(f32[16,1024]{1,0:T(8,128)} %get-tuple-element.26) | copy-start | bytes 196612
  69.0 13.9 %copy-start = (f32[16,1024]{1,0:T(8,128)}, f32[16,1024]{1,0:T(8,128)S(1)}, u32[]{:S(2)}) copy-start(f32[16,1024]{1,0:T(8,128)S(1)} %add_add_fusion.refs_0_) | copy-start | bytes 196612
  69.0 13.9 %collective-permute-start.5 = (f32[16,1024]{1,0:T(8,128)S(1)}, f32[16,1024]{1,0:T(8,128)S(1)}, u32[]{:S(2)}, u32[]{:S(2)}) collective-permute-start(f32[16,1024]{1,0:T(8,128)S(1)} %add_add_fusion.refs_0_), channel_id=1, source_target_pairs={{0,24},{8,0},{16,8},{24,16},{1,25},{9,1},{17,9},{25,17},{2,26},{10... | collective-permute-start | bytes 196616 | tf_op jit(solution)/shard_map/ppermute | solution.py:537
  70.5 12.4 %collective-permute-start.4 = (f32[16,1024]{1,0:T(8,128)S(1)}, f32[16,1024]{1,0:T(8,128)S(1)}, u32[]{:S(2)}, u32[]{:S(2)}) collective-permute-start(f32[16,1024]{1,0:T(8,128)S(1)} %add_add_fusion.refs_0_), channel_id=1, source_target_pairs={{0,16},{8,24},{16,0},{24,8},{1,17},{9,25},{17,1},{25,9},{2,18},{10... | collective-permute-start | bytes 196616 | tf_op jit(solution)/shard_map/ppermute | solution.py:537
  71.6 11.3 %collective-permute-start.3 = (f32[16,1024]{1,0:T(8,128)S(1)}, f32[16,1024]{1,0:T(8,128)S(1)}, u32[]{:S(2)}, u32[]{:S(2)}) collective-permute-start(f32[16,1024]{1,0:T(8,128)S(1)} %add_add_fusion.refs_0_), channel_id=1, source_target_pairs={{0,8},{8,16},{16,24},{24,0},{1,9},{9,17},{17,25},{25,1},{2,10},{10... | collective-permute-start | bytes 196616 | tf_op jit(solution)/shard_map/ppermute | solution.py:537
  82.9 0.6 copy-start.2
  82.9 0.6 copy-start.3
  83.6 0.6 copy-start.4
